TPU v7x, 32 devices: a whole 2x2x4 slice. The times are simulated.
32 devices in a mesh: dp: 8 (over z, x), fsdp: 4 (over y, core).
Axes of the slice: x: 2, y: 2, z: 4, core: 2. Of those that a mesh axis runs over, the one named last changes fastest.
Arguments:
- tokens: bfloat16 [32768, 768], P(('dp', 'fsdp')), may hold values from -6 to 6
- masked_rows: int32 [32768], P(('dp', 'fsdp')), may hold values 0 or 1
- replace_ids: int32 [32768], P(('dp', 'fsdp')), may hold values from 0 to 767
- cotangent: bfloat16 [32768, 768], P(('dp', 'fsdp')), may hold values from -6 to 6
- qkv_weight: bfloat16 [768, 2304], P(None, 'fsdp'), may hold values from -0.3125 to 0.3125
- query_bias: bfloat16 [768], P('fsdp'), may hold values from -3 to 3
- value_bias: bfloat16 [768], P('fsdp'), may hold values from -3 to 3
- proj_weight: bfloat16 [768, 768], P(None, 'fsdp'), may hold values from -0.875 to 0.875
- proj_bias: bfloat16 [768], P('fsdp'), may hold values from -3 to 3
- first_gain: bfloat16 [768], P('fsdp'), may hold values from 0.5 to 1.5
- first_shift: bfloat16 [768], P('fsdp'), may hold values from -3 to 3
- inner_weight: bfloat16 [768, 3072], P(None, 'fsdp'), may hold values from -0.21875 to 0.21875
- inner_bias: bfloat16 [3072], P('fsdp'), may hold values from -3 to 3
- outer_weight: bfloat16 [3072, 768], P('fsdp'), may hold values from -0.109375 to 0.109375
- outer_bias: bfloat16 [768], P('fsdp'), may hold values from -3 to 3
- second_gain: bfloat16 [768], P('fsdp'), may hold values from 0.5 to 1.5
- second_shift: bfloat16 [768], P('fsdp'), may hold values from -3 to 3
- embed_table: bfloat16 [768, 768], P('fsdp'), may hold values from -6 to 6
Outputs:
- layer_out: bfloat16 [32768, 768], P(('dp', 'fsdp'))
- token_grad: float32 [32768, 768], P(('dp', 'fsdp'))
- qkv_weight_grad: float32 [768, 2304], P(None, 'fsdp')
- query_bias_grad: float32 [768], P('fsdp')
- value_bias_grad: float32 [768], P('fsdp')
- proj_weight_grad: float32 [768, 768], P(None, 'fsdp')
- proj_bias_grad: float32 [768], P('fsdp')
- first_gain_grad: float32 [768], P('fsdp')
- first_shift_grad: float32 [768], P('fsdp')
- inner_weight_grad: float32 [768, 3072], P(None, 'fsdp')
- inner_bias_grad: float32 [3072], P('fsdp')
- outer_weight_grad: float32 [3072, 768], P('fsdp')
- outer_bias_grad: float32 [768], P('fsdp')
- second_gain_grad: float32 [768], P('fsdp')
- second_shift_grad: float32 [768], P('fsdp')
- embed_table_grad: float32 [768, 768], P('fsdp')
All inputs are finite; a program needn't handle non-finite values. No bound on the sum of `masked_rows` on one device may be relied on, other than what follows from the above.
Results may differ from a plain program's by a relative error of at most 0.023.
Values may be sent and summed in bfloat16 or wider, within the bound.
A program may use at most 192 MiB of HBM per device.

v0:
```python
from functools import partial

import jax
import jax.numpy as jnp
from jax import lax
from jax.sharding import PartitionSpec as P

D = 768
HEADS = 12
HEAD = 64
TABLE = 768
SEQ = 512


norm_eps = 1e-05


def norm_rows(hidden, gain, shift):
    center = jnp.mean(hidden, axis=-1, keepdims=True)
    offset = hidden - center
    spread = jnp.mean(offset * offset, axis=-1, keepdims=True)
    return offset * lax.rsqrt(spread + norm_eps) * gain + shift


def norm_back(hidden, gain, shift, incoming):
    _, pull = jax.vjp(norm_rows, hidden, gain.astype(jnp.float32), shift.astype(jnp.float32))
    return pull(incoming)


def attend(page_qkv):
    queries = page_qkv[:, 0]
    keys = page_qkv[:, 1]
    values = page_qkv[:, 2]
    scores = jnp.einsum(
        "qhd,khd->hqk", queries, keys, preferred_element_type=jnp.float32
    ) * HEAD ** (-0.5)
    largest = jnp.max(scores, axis=-1, keepdims=True)
    raised = jnp.exp(scores - largest)
    expsum = jnp.sum(raised, axis=-1, keepdims=True)
    probs = (raised / expsum).astype(jnp.bfloat16)
    mixed = jnp.einsum("hqk,khd->qhd", probs, values, preferred_element_type=jnp.float32)
    return (mixed.reshape(page_qkv.shape[0], D), (largest + jnp.log(expsum))[..., 0])


def attend_back(inputs_all):
    page_qkv, logsum, page_grad = inputs_all
    queries = page_qkv[:, 0]
    keys = page_qkv[:, 1]
    values = page_qkv[:, 2]
    scale = HEAD ** (-0.5)
    scores = jnp.einsum("qhd,khd->hqk", queries, keys, preferred_element_type=jnp.float32) * scale
    probs = jnp.exp(scores - logsum[..., None])
    probs_low = probs.astype(jnp.bfloat16)
    grad_prob = jnp.einsum("qhd,khd->hqk", page_grad, values, preferred_element_type=jnp.float32)
    grad_prob = lax.optimization_barrier(grad_prob.astype(jnp.bfloat16)).astype(jnp.float32)
    center = jnp.sum(probs * grad_prob, axis=-1, keepdims=True)
    grad_raw = (scale * probs * (grad_prob - center)).astype(jnp.bfloat16)
    grad_query = jnp.einsum("hqk,khd->qhd", grad_raw, keys, preferred_element_type=jnp.float32)
    grad_key = jnp.einsum("hqk,qhd->khd", grad_raw, queries, preferred_element_type=jnp.float32)
    grad_value = jnp.einsum(
        "hqk,qhd->khd", probs_low, page_grad, preferred_element_type=jnp.float32
    )
    stacked = jnp.stack([grad_query, grad_key, grad_value], axis=1)
    return stacked.reshape(page_qkv.shape[0], 3 * D)


def forward(weights, tokens, chosen, onehot):
    (
        qkv_weight,
        query_bias,
        value_bias,
        proj_weight,
        proj_bias,
        first_gain,
        first_shift,
        inner_weight,
        inner_bias,
        outer_weight,
        outer_bias,
        second_gain,
        second_shift,
        embed_table,
    ) = weights
    embedded = jnp.dot(onehot, embed_table, preferred_element_type=jnp.float32)
    start = jnp.where(chosen, embedded, tokens.astype(jnp.float32))
    start_low = start.astype(jnp.bfloat16)
    qkv_bias = jnp.concatenate([query_bias, jnp.zeros_like(query_bias), value_bias]).astype(
        jnp.float32
    )
    qkv_low = (
        jnp.dot(start_low, qkv_weight, preferred_element_type=jnp.float32) + qkv_bias
    ).astype(jnp.bfloat16)
    pages = qkv_low.reshape(-1, SEQ, 3, HEADS, HEAD)
    mixed, logsum = lax.map(attend, pages)
    attended = mixed.reshape(-1, D).astype(jnp.bfloat16)
    projected = jnp.dot(
        attended, proj_weight, preferred_element_type=jnp.float32
    ) + proj_bias.astype(jnp.float32)
    hidden_one = start + projected
    first = norm_rows(hidden_one, first_gain.astype(jnp.float32), first_shift.astype(jnp.float32))
    first_low = first.astype(jnp.bfloat16)
    inner = jnp.dot(
        first_low, inner_weight, preferred_element_type=jnp.float32
    ) + inner_bias.astype(jnp.float32)
    active = jax.nn.gelu(inner, approximate=False).astype(jnp.bfloat16)
    outer = jnp.dot(active, outer_weight, preferred_element_type=jnp.float32) + outer_bias.astype(
        jnp.float32
    )
    hidden_two = first + outer
    return (start_low, qkv_low, logsum, attended, hidden_one, first_low, inner, active, hidden_two)


def local(
    tokens,
    masked_rows,
    replace_ids,
    cotangent,
    qkv_weight,
    query_bias,
    value_bias,
    proj_weight,
    proj_bias,
    first_gain,
    first_shift,
    inner_weight,
    inner_bias,
    outer_weight,
    outer_bias,
    second_gain,
    second_shift,
    embed_table,
):
    weights = (
        lax.all_gather(qkv_weight, "fsdp", axis=1, tiled=True),
        lax.all_gather(query_bias, "fsdp", axis=0, tiled=True),
        lax.all_gather(value_bias, "fsdp", axis=0, tiled=True),
        lax.all_gather(proj_weight, "fsdp", axis=1, tiled=True),
        lax.all_gather(proj_bias, "fsdp", axis=0, tiled=True),
        lax.all_gather(first_gain, "fsdp", axis=0, tiled=True),
        lax.all_gather(first_shift, "fsdp", axis=0, tiled=True),
        lax.all_gather(inner_weight, "fsdp", axis=1, tiled=True),
        lax.all_gather(inner_bias, "fsdp", axis=0, tiled=True),
        lax.all_gather(outer_weight, "fsdp", axis=0, tiled=True),
        lax.all_gather(outer_bias, "fsdp", axis=0, tiled=True),
        lax.all_gather(second_gain, "fsdp", axis=0, tiled=True),
        lax.all_gather(second_shift, "fsdp", axis=0, tiled=True),
        lax.all_gather(embed_table, "fsdp", axis=0, tiled=True),
    )
    chosen = masked_rows[:, None] > 0
    onehot = (replace_ids[:, None] == jnp.arange(TABLE, dtype=jnp.int32)[None, :]).astype(
        jnp.bfloat16
    )
    saved = forward(weights, tokens, chosen, onehot)
    layer_out = norm_rows(
        saved[8], weights[11].astype(jnp.float32), weights[12].astype(jnp.float32)
    ).astype(jnp.bfloat16)
    back_weights = (
        lax.all_gather(qkv_weight, "fsdp", axis=1, tiled=True),
        lax.all_gather(query_bias, "fsdp", axis=0, tiled=True),
        lax.all_gather(value_bias, "fsdp", axis=0, tiled=True),
        lax.all_gather(proj_weight, "fsdp", axis=1, tiled=True),
        lax.all_gather(proj_bias, "fsdp", axis=0, tiled=True),
        lax.all_gather(first_gain, "fsdp", axis=0, tiled=True),
        lax.all_gather(first_shift, "fsdp", axis=0, tiled=True),
        lax.all_gather(inner_weight, "fsdp", axis=1, tiled=True),
        lax.all_gather(inner_bias, "fsdp", axis=0, tiled=True),
        lax.all_gather(outer_weight, "fsdp", axis=0, tiled=True),
        lax.all_gather(outer_bias, "fsdp", axis=0, tiled=True),
        lax.all_gather(second_gain, "fsdp", axis=0, tiled=True),
        lax.all_gather(second_shift, "fsdp", axis=0, tiled=True),
        lax.all_gather(embed_table, "fsdp", axis=0, tiled=True),
    )
    saved = forward(back_weights, tokens, chosen, onehot)
    start_low, qkv_low, logsum, attended, hidden_one, first_low, inner, active, hidden_two = saved
    (
        full_qkv,
        full_query_bias,
        full_value_bias,
        full_proj,
        full_proj_bias,
        full_first_gain,
        full_first_shift,
        full_inner,
        full_inner_bias,
        full_outer,
        full_outer_bias,
        full_second_gain,
        full_second_shift,
        full_table,
    ) = back_weights
    grad_out = jnp.where(chosen, cotangent.astype(jnp.float32), 0.0)
    grad_two, grad_second_gain, grad_second_shift = norm_back(
        hidden_two, full_second_gain, full_second_shift, grad_out
    )
    grad_outer_low = grad_two.astype(jnp.bfloat16)
    grad_outer_bias = jnp.sum(grad_outer_low, axis=0, dtype=jnp.float32)
    grad_outer_weight = jnp.dot(active.T, grad_outer_low, preferred_element_type=jnp.float32)
    grad_active = jnp.dot(grad_outer_low, full_outer.T, preferred_element_type=jnp.float32)
    _, gelu_pull = jax.vjp(partial(jax.nn.gelu, approximate=False), inner)
    grad_inner_low = gelu_pull(grad_active)[0].astype(jnp.bfloat16)
    grad_inner_bias = jnp.sum(grad_inner_low, axis=0, dtype=jnp.float32)
    grad_inner_weight = jnp.dot(first_low.T, grad_inner_low, preferred_element_type=jnp.float32)
    grad_first = grad_two + jnp.dot(
        grad_inner_low, full_inner.T, preferred_element_type=jnp.float32
    )
    grad_one, grad_first_gain, grad_first_shift = norm_back(
        hidden_one, full_first_gain, full_first_shift, grad_first
    )
    grad_proj_low = grad_one.astype(jnp.bfloat16)
    grad_proj_bias = jnp.sum(grad_proj_low, axis=0, dtype=jnp.float32)
    grad_proj_weight = jnp.dot(attended.T, grad_proj_low, preferred_element_type=jnp.float32)
    grad_attended = jnp.dot(grad_proj_low, full_proj.T, preferred_element_type=jnp.float32).astype(
        jnp.bfloat16
    )
    grad_pages = lax.map(
        attend_back,
        (
            qkv_low.reshape(-1, SEQ, 3, HEADS, HEAD),
            logsum,
            grad_attended.reshape(-1, SEQ, HEADS, HEAD),
        ),
    )
    grad_qkv_low = grad_pages.reshape(-1, 3 * D).astype(jnp.bfloat16)
    grad_query_bias = jnp.sum(grad_qkv_low[:, :D], axis=0, dtype=jnp.float32)
    grad_value_bias = jnp.sum(grad_qkv_low[:, 2 * D :], axis=0, dtype=jnp.float32)
    grad_qkv_weight = jnp.dot(start_low.T, grad_qkv_low, preferred_element_type=jnp.float32)
    grad_start = grad_one + jnp.dot(grad_qkv_low, full_qkv.T, preferred_element_type=jnp.float32)
    token_grad = jnp.where(chosen, 0.0, grad_start)
    grad_embed_low = jnp.where(chosen, grad_start, 0.0).astype(jnp.bfloat16)
    grad_table = jnp.dot(onehot.T, grad_embed_low, preferred_element_type=jnp.float32)
    shards = (
        lax.psum_scatter(
            grad_qkv_weight.astype(jnp.bfloat16), "fsdp", scatter_dimension=1, tiled=True
        ).astype(jnp.float32),
        lax.psum_scatter(
            grad_query_bias.astype(jnp.bfloat16), "fsdp", scatter_dimension=0, tiled=True
        ).astype(jnp.float32),
        lax.psum_scatter(
            grad_value_bias.astype(jnp.bfloat16), "fsdp", scatter_dimension=0, tiled=True
        ).astype(jnp.float32),
        lax.psum_scatter(
            grad_proj_weight.astype(jnp.bfloat16), "fsdp", scatter_dimension=1, tiled=True
        ).astype(jnp.float32),
        lax.psum_scatter(
            grad_proj_bias.astype(jnp.bfloat16), "fsdp", scatter_dimension=0, tiled=True
        ).astype(jnp.float32),
        lax.psum_scatter(
            grad_first_gain.astype(jnp.bfloat16), "fsdp", scatter_dimension=0, tiled=True
        ).astype(jnp.float32),
        lax.psum_scatter(
            grad_first_shift.astype(jnp.bfloat16), "fsdp", scatter_dimension=0, tiled=True
        ).astype(jnp.float32),
        lax.psum_scatter(
            grad_inner_weight.astype(jnp.bfloat16), "fsdp", scatter_dimension=1, tiled=True
        ).astype(jnp.float32),
        lax.psum_scatter(
            grad_inner_bias.astype(jnp.bfloat16), "fsdp", scatter_dimension=0, tiled=True
        ).astype(jnp.float32),
        lax.psum_scatter(
            grad_outer_weight.astype(jnp.bfloat16), "fsdp", scatter_dimension=0, tiled=True
        ).astype(jnp.float32),
        lax.psum_scatter(
            grad_outer_bias.astype(jnp.bfloat16), "fsdp", scatter_dimension=0, tiled=True
        ).astype(jnp.float32),
        lax.psum_scatter(
            grad_second_gain.astype(jnp.bfloat16), "fsdp", scatter_dimension=0, tiled=True
        ).astype(jnp.float32),
        lax.psum_scatter(
            grad_second_shift.astype(jnp.bfloat16), "fsdp", scatter_dimension=0, tiled=True
        ).astype(jnp.float32),
        lax.psum_scatter(
            grad_table.astype(jnp.bfloat16), "fsdp", scatter_dimension=0, tiled=True
        ).astype(jnp.float32),
    )
    summed = (
        lax.psum(shards[0].astype(jnp.bfloat16), "dp").astype(jnp.float32),
        lax.psum(shards[1].astype(jnp.bfloat16), "dp").astype(jnp.float32),
        lax.psum(shards[2].astype(jnp.bfloat16), "dp").astype(jnp.float32),
        lax.psum(shards[3].astype(jnp.bfloat16), "dp").astype(jnp.float32),
        lax.psum(shards[4].astype(jnp.bfloat16), "dp").astype(jnp.float32),
        lax.psum(shards[5].astype(jnp.bfloat16), "dp").astype(jnp.float32),
        lax.psum(shards[6].astype(jnp.bfloat16), "dp").astype(jnp.float32),
        lax.psum(shards[7].astype(jnp.bfloat16), "dp").astype(jnp.float32),
        lax.psum(shards[8].astype(jnp.bfloat16), "dp").astype(jnp.float32),
        lax.psum(shards[9].astype(jnp.bfloat16), "dp").astype(jnp.float32),
        lax.psum(shards[10].astype(jnp.bfloat16), "dp").astype(jnp.float32),
        lax.psum(shards[11].astype(jnp.bfloat16), "dp").astype(jnp.float32),
        lax.psum(shards[12].astype(jnp.bfloat16), "dp").astype(jnp.float32),
        lax.psum(shards[13].astype(jnp.bfloat16), "dp").astype(jnp.float32),
    )
    return (
        layer_out,
        token_grad,
        summed[0],
        summed[1],
        summed[2],
        summed[3],
        summed[4],
        summed[5],
        summed[6],
        summed[7],
        summed[8],
        summed[9],
        summed[10],
        summed[11],
        summed[12],
        summed[13],
    )


def solution(mesh):
    return jax.shard_map(
        local,
        mesh=mesh,
        in_specs=(
            P(("dp", "fsdp"), None),
            P(("dp", "fsdp")),
            P(("dp", "fsdp")),
            P(("dp", "fsdp"), None),
            P(None, "fsdp"),
            P("fsdp"),
            P("fsdp"),
            P(None, "fsdp"),
            P("fsdp"),
            P("fsdp"),
            P("fsdp"),
            P(None, "fsdp"),
            P("fsdp"),
            P("fsdp", None),
            P("fsdp"),
            P("fsdp"),
            P("fsdp"),
            P("fsdp", None),
        ),
        out_specs=(
            P(("dp", "fsdp"), None),
            P(("dp", "fsdp"), None),
            P(None, "fsdp"),
            P("fsdp"),
            P("fsdp"),
            P(None, "fsdp"),
            P("fsdp"),
            P("fsdp"),
            P("fsdp"),
            P(None, "fsdp"),
            P("fsdp"),
            P("fsdp", None),
            P("fsdp"),
            P("fsdp"),
            P("fsdp"),
            P("fsdp", None),
        ),
        check_vma=False,
    )
```

profile of v0, /device:TPU:0, one launch (start us, length us, event | category | flops | bytes accessed | tf_op | source)
XLA Modules:
  0.0 618.3 jit_solution(17767043599996172981)
XLA Ops:
  16.0 13.3 %all-reduce.20 = (bf16[768]{0:T(1024)(128)(2,1)S(1)}, bf16[768]{0:T(1024)(128)(2,1)S(1)}, bf16[768]{0:T(1024)(128)(2,1)S(1)}, bf16[768]{0:T(1024)(128)(2,1)S(1)}...) all-reduce(bf16[768]{0:T(1024)(128)(2,1)S(1)} %dynamic-update-slice, ...), channel_id=1, replica_groups=mesh['dp'=8,'fsdp'=4] {'fsdp'}, use_global_device_ids=true, to_apply=%add.1 | all-reduce | flops 5376 | bytes 21504
  30.5 5.2 all-gather
  39.2 5.6 convert_select_fusion.1
  44.7 17.7 %all-gather.9.cloned.1.call-done = bf16[768,2304]{0,1:T(8,128)(2,1)} async-done(((bf16[768,576]{0,1:T(8,128)(2,1)}), bf16[768,2304]{0,1:T(8,128)(2,1)}) %all-gather.9.cloned.1.call-update) | async-done | bytes 3538960 | tf_op jit(solution)/shard_map/all_gather | solution.py:134
  62.5 9.0 %add_convert_fusion.1 = bf16[1024,2304]{1,0:T(8,128)(2,1)} fusion(bf16[768,2304]{0,1:T(8,128)(2,1)} %all-gather.9.cloned.1.call-done, f32[2304]{0:T(1024)S(1)} %maximum_convert_fusion, f32[1024,768]{0,1:T(8,128)} %convert_select_fusion.1), kind=kOutput, calls=%fused_computation.93 | convolution fusion | flops 3629383680 | bytes 11412480 | tf_op jit(solution)/shard_map/dot_general | solution.py:91
  71.4 6.6 %copy.78 = bf16[1024,2304]{0,1:T(8,128)(2,1)} copy(bf16[1024,2304]{1,0:T(8,128)(2,1)} %add_convert_fusion.1) | data formatting | bytes 9437184 | tf_op jit(solution)/shard_map/convert_element_type | solution.py:92
  78.1 8.8 %reshape.193 = bf16[2,512,3,12,64]{1,0,4,3,2:T(2,128)(2,1)} reshape(bf16[1024,2304]{0,1:T(8,128)(2,1)} %copy.78) | data formatting | bytes 9437184 | tf_op jit(solution)/shard_map/reshape | solution.py:93
  86.9 6.0 copy.79
  93.0 18.3 %while.33 = (s32[]{:T(128)}, bf16[2,512,768]{2,1,0:T(8,128)(2,1)S(1)}, f32[2,12,512]{2,1,0:T(8,128)S(1)}, bf16[2,512,3,12,64]{1,4,3,2,0:T(8,128)(2,1)}, s32[]{:T(128)}) while((s32[]{:T(128)}, bf16[2,512,768]{2,1,0:T(8,128)(2,1)S(1)}, f32[2,12,512]{2,1,0:T(8,128)S(1)}, bf16[2,512,3,12,64]{1,4,3,2,0:T(8,128)(2,1)}, s32[]{:T(128)}) %tuple.94), condition=%wide.region_11.12_spmd, body=%wide.region_8.11_spmd.sunk | while | flops 833611776 | bytes 48996424 | solution.py:94
  95.2 1.8 multiply_reduce_fusion.11
  97.0 2.1 fusion.181
  99.2 2.8 fusion.182
  106.0 2.1 fusion.181
  108.2 2.8 fusion.182
  112.5 4.2 fusion.120
  117.2 3.3 all-gather.13.cloned.1.call-done
  120.4 38.0 %multiply_convert_fusion = (bf16[1024,3072]{1,0:T(8,128)(2,1)}, f32[1024,3072]{1,0:T(8,128)}, f32[1024,3072]{1,0:T(8,128)}) fusion(f32[3072]{0:T(1024)S(1)} %bitcast.194, bf16[768,3072]{1,0:T(8,128)(2,1)} %all-gather.13.cloned.1.call-done, f32[1024,768]{0,1:T(8,128)S(1)} %get-tuple-element.257, f32[1024]{0:T(1024)S(1)} %fusion.76, ...), kind=kOutput, calls=%fused_computation.64 | convolution fusion | flops 5043388416 | bytes 39348224 | tf_op jit(solution)/shard_map/dot_general | solution.py:102
  159.3 9.7 %fusion.121 = (f32[1024]{0:T(1024)S(1)}, f32[1024,768]{0,1:T(8,128)S(1)}) fusion(f32[768]{0:T(1024)S(1)} %copy-done.44, bf16[1024,3072]{1,0:T(8,128)(2,1)} %get-tuple-element.242, bf16[3072,768]{1,0:T(8,128)(2,1)} %all-gather.15.cloned.1.call-done, f32[768]{0:T(1024)S(1)} %copy-done.42, f32[768]{0:T(1024)S(1)} %copy-done.24, f32[1024]{0:T(1024)S(1)} %fusion.76, ...), kind=kOutput, calls=%fused_computation.203 | convolution fusion | flops 4837342208 | bytes 17323008 | tf_op jit(solution)/shard_map/dot_general | solution.py:106
  170.8 2.0 multiply_reduce_fusion.2
  172.8 1.9 fusion.113
  174.7 18.2 %fusion.122 = (bf16[3072]{0:T(1024)(128)(2,1)}, bf16[1024,3072]{1,0:T(8,128)(2,1)}) fusion(f32[1024,3072]{1,0:T(8,128)} %get-tuple-element.243, bf16[1024,768]{0,1:T(8,128)(2,1)S(1)} %get-tuple-element.237, bf16[3072,768]{1,0:T(8,128)(2,1)} %all-gather.15.cloned.1.call-done, f32[1024,3072]{1,0:T(8,128)} %get-tuple-element.258, f32[3072]{0:T(1024)S(1)} %bitcast.195), kind=kOutput, calls=%fused_computation.204 | convolution fusion | flops 4882166784 | bytes 37767168 | tf_op jit(solution)/shard_map/dot_general | solution.py:198
  192.9 11.7 %multiply_reduce_fusion.3 = (bf16[768]{0:T(1024)(128)(2,1)}, f32[1024]{0:T(1024)S(1)}, bf16[768]{0:T(1024)(128)(2,1)}, f32[1024,768]{0,1:T(8,128)S(1)}) fusion(f32[1024,768]{0,1:T(8,128)} %copy-done.3, f32[1024]{0:T(1024)S(1)} %fusion.76, f32[1024]{0:T(1024)S(1)} %broadcast_multiply_fusion.1, f32[768]{0:T(1024)S(1)} %copy-done.24, ...), kind=kOutput, calls=%fused_computation.102 | convolution fusion | flops 4845990912 | bytes 22059008 | tf_op jit(solution)/shard_map/dot_general | solution.py:203
  208.0 2.4 convolution_convert_fusion.5
  210.5 2.7 convolution_convert_fusion.4
  214.4 2.4 reshape.194
  216.7 1.9 copy.87
  218.7 47.8 %while.34 = (s32[]{:T(128)}, bf16[2,512,2304]{2,1,0:T(8,128)(2,1)}, bf16[2,512,3,12,64]{1,4,3,2,0:T(8,128)(2,1)}, f32[2,12,512]{2,1,0:T(8,128)S(1)}, bf16[2,512,12,64]{1,3,2,0:T(8,128)(2,1)S(1)}, /*index=5*/s32[]{:T(128)}) while((s32[]{:T(128)}, bf16[2,512,2304]{2,1,0:T(8,128)(2,1)}, bf16[2,512,3,12,64]{1,4,3,2,0:T(8,128)(2,1)}, ...), condition=%wide.region_22.23_spmd, body=%wide.region_20.22_spmd.sunk | while | flops 2065950720 | bytes 115008144 | solution.py:215
  218.7 2.5 dynamic-slice_bitcast_fusion.10
  223.1 4.2 fusion.188
  227.3 3.5 fusion.190
  232.0 2.0 convolution_bitcast_fusion.4
  234.0 2.4 fusion.189
  236.7 2.4 copy.127
  239.1 3.4 constant_dynamic-update-slice_fusion.8
  242.5 2.5 dynamic-slice_bitcast_fusion.10
  246.9 4.2 fusion.188
  251.1 3.5 fusion.190
  255.8 2.0 convolution_bitcast_fusion.4
  257.8 2.4 fusion.189
  260.5 2.4 copy.127
  262.9 3.3 constant_dynamic-update-slice_fusion.8
  266.5 10.0 %broadcast_select_fusion = (f32[1024,768]{0,1:T(8,128)}, bf16[1024,768]{0,1:T(8,128)(2,1)S(1)}) fusion(pred[1024]{0:T(1024)(128)(4,1)S(1)} %copy-done.32, bf16[1024,2304]{1,0:T(8,128)(2,1)} %bitcast.188, bf16[768,2304]{0,1:T(8,128)(2,1)} %all-gather.9.cloned.1.call-done, f32[1024,768]{0,1:T(8,128)} %copy-done.6, f32[1024]{0:T(1024)S(1)} %copy-done.29), kind=kOutput, calls=%fused_computation.135 | convolution fusion | flops 3627024384 | bytes 16126976 | tf_op jit(solution)/shard_map/dot_general | solution.py:227
  276.4 2.7 fusion.71
  279.2 9.0 %convolution_convert_fusion.3 = bf16[768,2304]{0,1:T(8,128)(2,1)} fusion(bf16[1024,2304]{1,0:T(8,128)(2,1)} %bitcast.189, f32[1024,768]{0,1:T(8,128)} %convert_select_fusion.1), kind=kOutput, calls=%fused_computation.97 | convolution fusion | flops 3626434560 | bytes 11403264 | tf_op jit(solution)/shard_map/dot_general | solution.py:226
  288.3 9.7 %convolution_convert_fusion.1 = bf16[3072,768]{1,0:T(8,128)(2,1)} fusion(bf16[1024,3072]{1,0:T(8,128)(2,1)} %get-tuple-element.242, bf16[1024,768]{0,1:T(8,128)(2,1)S(1)} %copy-done.14), kind=kOutput, calls=%fused_computation.95 | convolution fusion | flops 4834197504 | bytes 12582912 | tf_op jit(solution)/shard_map/dot_general | solution.py:197
  299.9 10.2 %convolution_convert_fusion.2 = bf16[768,3072]{1,0:T(8,128)(2,1)} fusion(bf16[1024,3072]{1,0:T(8,128)(2,1)} %get-tuple-element.263, f32[1024,768]{0,1:T(8,128)S(1)} %copy-done.5, f32[1024]{0:T(1024)S(1)} %copy-done.27, f32[1024]{0:T(1024)S(1)} %copy-done.23, f32[768]{0:T(1024)S(1)} %copy-done.43, f32[768]{0:T(1024)S(1)} %copy-done.25), kind=kOutput, calls=%fused_computation.96 | convolution fusion | flops 4838129664 | bytes 14170112 | tf_op jit(solution)/shard_map/dot_general | solution.py:202
  313.0 32.5 %while.32 = (s32[]{:T(128)}, bf16[2,512,768]{2,1,0:T(8,128)(2,1)}, bf16[2,512,3,12,64]{1,4,3,2,0:T(8,128)(2,1)}, s32[]{:T(128)}) while((s32[]{:T(128)}, bf16[2,512,768]{2,1,0:T(8,128)(2,1)}, bf16[2,512,3,12,64]{1,4,3,2,0:T(8,128)(2,1)}, s32[]{:T(128)}) %tuple.124), condition=%wide.region_3.4_spmd, body=%wide.region_0.3_spmd.sunk | while | flops 821035520 | bytes 36233784 | solution.py:94
  313.0 1.9 dynamic-slice_bitcast_fusion.8
  314.9 7.0 %fusion.179 = (f32[12,512]{1,0:T(8,128)S(1)}, f32[12,512,512]{1,2,0:T(8,128)}) fusion(bf16[512,3,12,64]{0,3,2,1:T(8,128)(2,1)S(1)} %dynamic-slice_bitcast_fusion.8), kind=kOutput, calls=%fused_computation.199.clone.1 | convolution fusion | flops 412090880 | bytes 14180352 | tf_op jit(solution)/shard_map/while/body/eval_jaxpr/sub | solution.py:38
  321.9 6.4 %fusion.180 = bf16[12,64,512]{2,1,0:T(8,128)(2,1)S(1)} fusion(f32[12,512,512]{1,2,0:T(8,128)} %get-tuple-element.342, f32[12,512]{1,0:T(8,128)S(1)} %get-tuple-element.343, bf16[512,3,12,64]{0,3,2,1:T(8,128)(2,1)S(1)} %dynamic-slice_bitcast_fusion.8), kind=kOutput, calls=%fused_computation.6.clone.1 | convolution fusion | flops 408944640 | bytes 14188544 | tf_op jit(solution)/shard_map/while/body/eval_jaxpr/hqk,khd->qhd/dot_general | solution.py:41
  331.4 7.0 %fusion.179 = (f32[12,512]{1,0:T(8,128)S(1)}, f32[12,512,512]{1,2,0:T(8,128)}) fusion(bf16[512,3,12,64]{0,3,2,1:T(8,128)(2,1)S(1)} %dynamic-slice_bitcast_fusion.8), kind=kOutput, calls=%fused_computation.199.clone.1 | convolution fusion | flops 412090880 | bytes 14180352 | tf_op jit(solution)/shard_map/while/body/eval_jaxpr/sub | solution.py:38
  338.4 5.8 fusion.180
  345.4 4.2 fusion.119
  350.1 48.4 %reduce-scatter.12.cloned.1.call-done = bf16[768,768]{1,0:T(8,128)(2,1)} async-done(((bf16[3072,768]{1,0:T(8,128)(2,1)}), bf16[768,768]{1,0:T(8,128)(2,1)}) %reduce-scatter.12.cloned.1.call-update) | async-done | bytes 1179664 | tf_op jit(solution)/shard_map/reduce_scatter | solution.py:259
  398.5 50.2 %reduce-scatter.10.cloned.1.call-done = bf16[768,768]{1,0:T(8,128)(2,1)} async-done(((bf16[768,3072]{1,0:T(8,128)(2,1)}), bf16[768,768]{1,0:T(8,128)(2,1)}) %reduce-scatter.10.cloned.1.call-update) | async-done | bytes 1179664 | tf_op jit(solution)/shard_map/reduce_scatter | solution.py:253
  448.9 35.7 %fusion.58.clone.4 = bf16[1024,3072]{1,0:T(8,128)(2,1)} fusion(f32[3072]{0:T(1024)S(1)} %bitcast.196, bf16[768,3072]{1,0:T(8,128)(2,1)} %all-gather.13.cloned.1.call-done, f32[1024,768]{0,1:T(8,128)S(1)} %get-tuple-element.255, f32[768]{0:T(1024)S(1)} %copy-done.43, f32[768]{0:T(1024)S(1)} %copy-done.25, ...), kind=kOutput, calls=%fused_computation.61.clone.clone.clone.clone.clone.clone.1 | convolution fusion | flops 5043388416 | bytes 14182400 | tf_op jit(solution)/shard_map/dot_general | solution.py:102
  484.7 2.5 slice_reduce_fusion
  487.3 11.1 %all-reduce.19 = (bf16[768]{0:T(1024)(128)(2,1)S(1)}, bf16[768]{0:T(1024)(128)(2,1)S(1)}, bf16[768]{0:T(1024)(128)(2,1)S(1)}, bf16[768]{0:T(1024)(128)(2,1)S(1)}...) all-reduce(bf16[768]{0:T(1024)(128)(2,1)S(1)} %copy-done.40, ...), channel_id=1, replica_groups=mesh['dp'=8,'fsdp'=4] {'fsdp'}, use_global_device_ids=true, to_apply=%add.7 | all-reduce | flops 9984 | bytes 39936
  499.0 21.7 %all-reduce.17 = (bf16[192]{0:T(256)(128)(2,1)S(1)}, bf16[192]{0:T(256)(128)(2,1)S(1)}, bf16[192]{0:T(256)(128)(2,1)S(1)}, bf16[192]{0:T(256)(128)(2,1)S(1)}, bf...) all-reduce(bf16[192]{0:T(256)(128)(2,1)S(1)} %dynamic-slice.9, ...), channel_id=1, replica_groups=mesh['dp'=8,'fsdp'=4] {'dp'}, use_global_device_ids=true, to_apply=%region_27.28 | all-reduce | flops 2304 | bytes 9216 | tf_op jit(solution)/shard_map/psum | solution.py:277
  525.9 2.4 copy.91
  528.2 9.4 %fusion.123 = (f32[1024]{0:T(1024)S(1)}, f32[1024,768]{0,1:T(8,128)S(1)}) fusion(f32[768]{0:T(1024)S(1)} %copy-done.45, bf16[3072,768]{1,0:T(8,128)(2,1)} %all-gather.15.cloned.1.call-done, f32[768]{0:T(1024)S(1)} %copy-done.43, f32[768]{0:T(1024)S(1)} %copy-done.25, f32[1024]{0:T(1024)S(1)} %add_rsqrt_fusion.1, f32[1024,768]{0,1:T(8,128)} %copy-done.8, ...), kind=kOutput, calls=%fused_computation.205 | convolution fusion | flops 4837342208 | bytes 17323008 | tf_op jit(solution)/shard_map/dot_general | solution.py:106
  540.2 62.6 %all-reduce.23.cloned.1.call-done = (bf16[768,576]{0,1:T(8,128)(2,1)}, bf16[768,192]{0,1:T(8,128)(2,1)}, bf16[768,768]{1,0:T(8,128)(2,1)}, bf16[768,768]{1,0:T(8,128)(2,1)}, bf16[192,768]{1,0:T(8,128)(2,1)}) async-done(((bf16[768,576]{0,1:T(8,128)(2,1)}, bf16[768,192]{0,1:T(8,128)(2,1)}, bf16[768,768]{1,0:T(8,128)(2,1)}, bf16[768,768]{1,0:T(8,128)(2,1)}, bf16[192,768]{1,0:T(8,128)(2,1)}), ...) | async-done | bytes 3833872 | tf_op jit(solution)/shard_map/psum | solution.py:276
  602.7 3.0 convert_element_type.264
  605.7 2.8 convert_element_type.267
  (253 shorter events, 53.7 us)
Async XLA Ops:
  7.2 5.9 copy-start.50
  7.2 4.3 copy-start.9
  7.2 7.1 %copy-start.54 = (bf16[192]{0:T(256)(128)(2,1)S(1)}, bf16[192]{0:T(256)(128)(2,1)}, u32[]{:S(2)}) copy-start(bf16[192]{0:T(256)(128)(2,1)} %param.29) | copy-start | bytes 1156
  7.2 7.4 %copy-start.55 = (bf16[192]{0:T(256)(128)(2,1)S(1)}, bf16[192]{0:T(256)(128)(2,1)}, u32[]{:S(2)}) copy-start(bf16[192]{0:T(256)(128)(2,1)} %param.30) | copy-start | bytes 1156
  7.2 7.6 %copy-start.56 = (bf16[192]{0:T(256)(128)(2,1)S(1)}, bf16[192]{0:T(256)(128)(2,1)}, u32[]{:S(2)}) copy-start(bf16[192]{0:T(256)(128)(2,1)} %param.32) | copy-start | bytes 1156
  7.2 7.8 %copy-start.57 = (bf16[192]{0:T(256)(128)(2,1)S(1)}, bf16[192]{0:T(256)(128)(2,1)}, u32[]{:S(2)}) copy-start(bf16[192]{0:T(256)(128)(2,1)} %param.33) | copy-start | bytes 1156
  7.2 8.1 %copy-start.58 = (bf16[192]{0:T(256)(128)(2,1)S(1)}, bf16[192]{0:T(256)(128)(2,1)}, u32[]{:S(2)}) copy-start(bf16[192]{0:T(256)(128)(2,1)} %param.34) | copy-start | bytes 1156
  7.3 8.3 %copy-start.59 = (bf16[192]{0:T(256)(128)(2,1)S(1)}, bf16[192]{0:T(256)(128)(2,1)}, u32[]{:S(2)}) copy-start(bf16[192]{0:T(256)(128)(2,1)} %param.38) | copy-start | bytes 1156
  7.3 8.5 %copy-start.60 = (bf16[192]{0:T(256)(128)(2,1)S(1)}, bf16[192]{0:T(256)(128)(2,1)}, u32[]{:S(2)}) copy-start(bf16[192]{0:T(256)(128)(2,1)} %param.39) | copy-start | bytes 1156
  7.3 23.2 %copy-start.51 = (bf16[768]{0:T(1024)(128)(2,1)S(1)}, bf16[768]{0:T(1024)(128)(2,1)}, u32[]{:S(2)}) copy-start(bf16[768]{0:T(1024)(128)(2,1)} %param.36) | copy-start | bytes 4612
  7.3 30.2 %copy-start.10 = (bf16[1024,768]{1,0:T(8,128)(2,1)S(1)}, bf16[1024,768]{1,0:T(8,128)(2,1)}, u32[]{:S(2)}) copy-start(bf16[1024,768]{1,0:T(8,128)(2,1)} %param.27) | copy-start | bytes 4718596
  7.3 31.8 %all-gather.7.cloned.1.call-start = ((), (), s32[]{:S(2)}) async-start(), calls=%async_computation.5 | async-start | bytes 1474560 | tf_op jit(solution)/shard_map/all_gather | solution.py:147
  8.0 54.4 %all-gather.9.cloned.1.call-start = ((), (), s32[]{:S(2)}) async-start(), calls=%async_computation.6 | async-start | bytes 4423680 | tf_op jit(solution)/shard_map/all_gather | solution.py:134
  8.8 30.4 %copy-start.52 = (s32[1024]{0:T(1024)S(1)}, s32[1024]{0:T(1024)}, u32[]{:S(2)}) copy-start(s32[1024]{0:T(1024)} %param.26) | copy-start | bytes 12292
  8.8 102.6 %all-gather.11.cloned.1.call-start = ((), (), s32[]{:S(2)}) async-start(), calls=%async_computation.7 | async-start | bytes 1474560 | tf_op jit(solution)/shard_map/all_gather | solution.py:137
  9.5 110.9 %all-gather.13.cloned.1.call-start = ((), (), s32[]{:S(2)}) async-start(), calls=%async_computation.8 | async-start | bytes 5898240 | tf_op jit(solution)/shard_map/all_gather | solution.py:141
  10.1 149.2 %all-gather.15.cloned.1.call-start = ((), (), s32[]{:S(2)}) async-start(), calls=%async_computation.9 | async-start | bytes 5898240 | tf_op jit(solution)/shard_map/all_gather | solution.py:143
  10.7 339.4 %reduce-scatter.8.cloned.1.call-start = ((), (), s32[]{:S(2)}) async-start(), calls=%async_computation.11 | async-start | bytes 1474560 | tf_op jit(solution)/shard_map/reduce_scatter | solution.py:241
  11.5 33.3 %copy-start.30 = (pred[1024]{0:T(1024)(128)(4,1)}, pred[1024]{0:T(1024)(128)(4,1)S(1)}, u32[]{:S(2)}) copy-start(pred[1024]{0:T(1024)(128)(4,1)S(1)} %broadcast_compare_fusion) | copy-start | bytes 3076
  29.3 83.1 %copy-start.46 = (f32[768]{0:T(1024)}, f32[768]{0:T(1024)S(1)}, u32[]{:S(2)}) copy-start(f32[768]{0:T(1024)S(1)} %convert_element_type.231) | copy-start | bytes 9220
  111.4 5.4 copy-start.16
  112.5 7.9 %copy-start.24 = (f32[768]{0:T(1024)S(1)}, f32[768]{0:T(1024)}, u32[]{:S(2)}) copy-start(f32[768]{0:T(1024)} %convert_element_type.232) | copy-start | bytes 9220
  112.5 7.9 %copy-start.33 = (f32[4,1,768]{2,1,0:T(1,128)S(1)}, f32[4,1,768]{2,1,0:T(1,128)}, u32[]{:S(2)}) copy-start(f32[4,1,768]{2,1,0:T(1,128)} %convert_element_type.276) | copy-start | bytes 36868
  112.5 7.9 %copy-start.42 = (f32[768]{0:T(1024)S(1)}, f32[768]{0:T(1024)}, u32[]{:S(2)}) copy-start(f32[768]{0:T(1024)} %convert_element_type.233) | copy-start | bytes 9220
  116.7 41.7 %copy-start.3 = (f32[1024,768]{0,1:T(8,128)}, f32[1024,768]{0,1:T(8,128)S(1)}, u32[]{:S(2)}) copy-start(f32[1024,768]{0,1:T(8,128)S(1)} %get-tuple-element.257) | copy-start | bytes 9437188
  116.8 87.9 %copy-start.22 = (f32[1024]{0:T(1024)}, f32[1024]{0:T(1024)S(1)}, u32[]{:S(2)}) copy-start(f32[1024]{0:T(1024)S(1)} %broadcast_multiply_fusion.1) | copy-start | bytes 12292
  117.2 87.5 %copy-start.26 = (f32[1024]{0:T(1024)}, f32[1024]{0:T(1024)S(1)}, u32[]{:S(2)}) copy-start(f32[1024]{0:T(1024)S(1)} %fusion.76) | copy-start | bytes 12292
  120.4 38.9 %copy-start.44 = (f32[768]{0:T(1024)S(1)}, f32[768]{0:T(1024)}, u32[]{:S(2)}) copy-start(f32[768]{0:T(1024)} %convert_element_type.237) | copy-start | bytes 9220
  159.3 9.7 %copy-start.2 = (bf16[1024,768]{0,1:T(8,128)(2,1)S(1)}, bf16[1024,768]{0,1:T(8,128)(2,1)}, u32[]{:S(2)}) copy-start(bf16[1024,768]{0,1:T(8,128)(2,1)} %copy.81) | copy-start | bytes 4718596
  159.3 9.7 %copy-start.20 = (f32[768]{0:T(1024)S(1)}, f32[768]{0:T(1024)}, u32[]{:S(2)}) copy-start(f32[768]{0:T(1024)} %convert_element_type.238) | copy-start | bytes 9220
  159.3 9.7 %copy-start.31 = (pred[1024]{0:T(1024)(128)(4,1)S(1)}, pred[1024]{0:T(1024)(128)(4,1)}, u32[]{:S(2)}) copy-start(pred[1024]{0:T(1024)(128)(4,1)} %copy-done.30) | copy-start | bytes 3076
  174.7 18.2 %copy-start.13 = (bf16[1024,768]{0,1:T(8,128)(2,1)}, bf16[1024,768]{0,1:T(8,128)(2,1)S(1)}, u32[]{:S(2)}) copy-start(bf16[1024,768]{0,1:T(8,128)(2,1)S(1)} %get-tuple-element.237) | copy-start | bytes 4718596
  192.9 11.7 %copy-start.4 = (f32[1024,768]{0,1:T(8,128)S(1)}, f32[1024,768]{0,1:T(8,128)}, u32[]{:S(2)}) copy-start(f32[1024,768]{0,1:T(8,128)} %copy-done.3) | copy-start | bytes 9437188
  210.4 139.7 %reduce-scatter.14.cloned.1.call-start = ((), (), s32[]{:S(2)}) async-start(), calls=%async_computation.14 | async-start | bytes 1474560 | tf_op jit(solution)/shard_map/reduce_scatter | solution.py:271
  213.2 5.4 copy-start.17
  218.6 47.8 %copy-start.29 = (f32[1024]{0:T(1024)S(1)}, f32[1024]{0:T(1024)}, u32[]{:S(2)}) copy-start(f32[1024]{0:T(1024)} %copy-done.28) | copy-start | bytes 12292
  218.6 47.8 %copy-start.32 = (pred[1024]{0:T(1024)(128)(4,1)S(1)}, pred[1024]{0:T(1024)(128)(4,1)}, u32[]{:S(2)}) copy-start(pred[1024]{0:T(1024)(128)(4,1)} %copy-done.30) | copy-start | bytes 3076
  218.7 15.3 %copy-start = (bf16[2,512,12,64]{1,3,2,0:T(8,128)(2,1)}, bf16[2,512,12,64]{1,3,2,0:T(8,128)(2,1)S(1)}, u32[]{:S(2)}) copy-start(bf16[2,512,12,64]{1,3,2,0:T(8,128)(2,1)S(1)} %get-tuple-element.400) | copy-start | bytes 4718596 | tf_op jit(solution)/shard_map/while
  239.1 3.4 copy-start.1
  242.5 15.3 %copy-start = (bf16[2,512,12,64]{1,3,2,0:T(8,128)(2,1)}, bf16[2,512,12,64]{1,3,2,0:T(8,128)(2,1)S(1)}, u32[]{:S(2)}) copy-start(bf16[2,512,12,64]{1,3,2,0:T(8,128)(2,1)S(1)} %get-tuple-element.400) | copy-start | bytes 4718596 | tf_op jit(solution)/shard_map/while
  262.9 3.3 copy-start.1
  266.4 10.0 %copy-start.53 = (s32[1024]{0:T(1024)S(1)}, s32[1024]{0:T(1024)}, u32[]{:S(2)}) copy-start(s32[1024]{0:T(1024)} %param.26) | copy-start | bytes 12292
  279.1 9.2 %copy-start.14 = (bf16[1024,768]{0,1:T(8,128)(2,1)S(1)}, bf16[1024,768]{0,1:T(8,128)(2,1)}, u32[]{:S(2)}) copy-start(bf16[1024,768]{0,1:T(8,128)(2,1)} %copy-done.13) | copy-start | bytes 4718596
  279.1 71.0 %reduce-scatter.6.cloned.1.call-start = ((), (), s32[]{:S(2)}) async-start(), calls=%async_computation.10 | async-start | bytes 4423680 | tf_op jit(solution)/shard_map/reduce_scatter | solution.py:232
  288.2 110.3 %reduce-scatter.12.cloned.1.call-start = ((), (), s32[]{:S(2)}) async-start(), calls=%async_computation.13 | async-start | bytes 5898240 | tf_op jit(solution)/shard_map/reduce_scatter | solution.py:259
  298.1 150.7 %reduce-scatter.10.cloned.1.call-start = ((), (), s32[]{:S(2)}) async-start(), calls=%async_computation.12 | async-start | bytes 5898240 | tf_op jit(solution)/shard_map/reduce_scatter | solution.py:253
  310.1 292.6 %all-reduce.23.cloned.1.call-start = ((), (), s32[]{:S(2)}) async-start(), calls=%async_computation.15 | async-start | bytes 7667712 | tf_op jit(solution)/shard_map/psum | solution.py:276
  313.0 32.5 %copy-start.47 = (f32[768]{0:T(1024)S(1)}, f32[768]{0:T(1024)}, u32[]{:S(2)}) copy-start(f32[768]{0:T(1024)} %copy-done.46) | copy-start | bytes 9220
  349.6 99.2 %copy-start.8 = (f32[1024,768]{0,1:T(8,128)}, f32[1024,768]{0,1:T(8,128)S(1)}, u32[]{:S(2)}) copy-start(f32[1024,768]{0,1:T(8,128)S(1)} %get-tuple-element.255) | copy-start | bytes 9437188
  349.6 99.2 %copy-start.34 = (f32[4,1,768]{2,1,0:T(1,128)S(1)}, f32[4,1,768]{2,1,0:T(1,128)}, u32[]{:S(2)}) copy-start(f32[4,1,768]{2,1,0:T(1,128)} %convert_element_type.276) | copy-start | bytes 36868
  448.8 38.4 %copy-start.35 = (bf16[768]{0:T(1024)(128)(2,1)S(1)}, bf16[768]{0:T(1024)(128)(2,1)}, u32[]{:S(2)}) copy-start(bf16[768]{0:T(1024)(128)(2,1)} %get-tuple-element.180) | copy-start | bytes 4612
  448.8 38.4 %copy-start.36 = (bf16[768]{0:T(1024)(128)(2,1)S(1)}, bf16[768]{0:T(1024)(128)(2,1)}, u32[]{:S(2)}) copy-start(bf16[768]{0:T(1024)(128)(2,1)} %get-tuple-element.238) | copy-start | bytes 4612
  448.9 38.4 %copy-start.37 = (bf16[768]{0:T(1024)(128)(2,1)S(1)}, bf16[768]{0:T(1024)(128)(2,1)}, u32[]{:S(2)}) copy-start(bf16[768]{0:T(1024)(128)(2,1)} %get-tuple-element.173) | copy-start | bytes 4612
  448.9 38.4 %copy-start.38 = (bf16[768]{0:T(1024)(128)(2,1)S(1)}, bf16[768]{0:T(1024)(128)(2,1)}, u32[]{:S(2)}) copy-start(bf16[768]{0:T(1024)(128)(2,1)} %get-tuple-element.236) | copy-start | bytes 4612
  448.9 38.4 %copy-start.40 = (bf16[768]{0:T(1024)(128)(2,1)S(1)}, bf16[768]{0:T(1024)(128)(2,1)}, u32[]{:S(2)}) copy-start(bf16[768]{0:T(1024)(128)(2,1)} %copy-done.39) | copy-start | bytes 4612
  448.9 38.4 %copy-start.41 = (bf16[3072]{0:T(1024)(128)(2,1)S(1)}, bf16[3072]{0:T(1024)(128)(2,1)}, u32[]{:S(2)}) copy-start(bf16[3072]{0:T(1024)(128)(2,1)} %get-tuple-element.262) | copy-start | bytes 18436
  448.9 38.4 %copy-start.48 = (bf16[768]{0:T(1024)(128)(2,1)S(1)}, bf16[768]{0:T(1024)(128)(2,1)}, u32[]{:S(2)}) copy-start(bf16[768]{0:T(1024)(128)(2,1)} %get-tuple-element.171) | copy-start | bytes 4612
  448.9 38.4 %copy-start.49 = (bf16[768]{0:T(1024)(128)(2,1)S(1)}, bf16[768]{0:T(1024)(128)(2,1)}, u32[]{:S(2)}) copy-start(bf16[768]{0:T(1024)(128)(2,1)} %get-tuple-element.179) | copy-start | bytes 4612
  484.7 41.2 %copy-start.7 = (f32[1024,768]{0,1:T(8,128)S(1)}, f32[1024,768]{0,1:T(8,128)}, u32[]{:S(2)}) copy-start(f32[1024,768]{0,1:T(8,128)} %get-tuple-element.266) | copy-start | bytes 9437188
  484.7 43.6 %copy-start.45 = (f32[768]{0:T(1024)S(1)}, f32[768]{0:T(1024)}, u32[]{:S(2)}) copy-start(f32[768]{0:T(1024)} %convert_element_type.237) | copy-start | bytes 9220
  528.2 9.9 %copy-start.21 = (f32[768]{0:T(1024)S(1)}, f32[768]{0:T(1024)}, u32[]{:S(2)}) copy-start(f32[768]{0:T(1024)} %convert_element_type.238) | copy-start | bytes 9220
  602.7 5.8 copy-start.15
  602.7 7.1 %copy-start.19 = (bf16[768,192]{0,1:T(8,128)(2,1)S(1)}, bf16[768,192]{0,1:T(8,128)(2,1)}, u32[]{:S(2)}) copy-start(bf16[768,192]{0,1:T(8,128)(2,1)} %get-tuple-element.215) | copy-start | bytes 884740
  602.7 8.0 %copy-start.18 = (bf16[192,768]{1,0:T(8,128)(2,1)S(1)}, bf16[192,768]{1,0:T(8,128)(2,1)}, u32[]{:S(2)}) copy-start(bf16[192,768]{1,0:T(8,128)(2,1)} %get-tuple-element.218) | copy-start | bytes 884740
  (11 other events, 19.9 us)
Sparse Core Ops, SparseCore 0:
  9.7 20.2 all-gather.6
  31.6 30.8 all-gather.8
  64.0 17.4 all-gather.10
  82.9 37.4 all-gather.12
  121.8 37.4 all-gather.14
  210.6 25.7 reduce-scatter.7
  279.2 25.6 reduce-scatter.13
  307.5 40.4 reduce-scatter.5
  350.7 47.8 reduce-scatter.11
  400.9 47.8 reduce-scatter.9
  453.6 149.0 all-reduce.22
where the time goes:
time: 627 us; the launch traced here: 618 us
  matrix products  251 us (40%)
  waiting for transfers between devices  186 us (30%)
  local copies, waits for them, and re-layouts  70.3 us (11%)
  blocking collectives  51.3 us (8%)
  other arithmetic  41 us (7%)
  between operations  16.8 us (3%)
    dot_general x2, matrix products, forward(): jnp.dot(first_low, inner_weight, preferred_element_type=jnp.float32)  73.8 us
    psum x1, waiting for transfers between devices, local(): lax.psum(shards[0].astype(jnp.bfloat16), 'dp').astype(jnp.float32)  62.6 us
    reduce_scatter x1, waiting for transfers between devices, local(): lax.psum_scatter(grad_inner_weight.astype(jnp.bfloat16), 'fsdp', scatter_...  50.2 us
    reduce_scatter x1, waiting for transfers between devices, local(): lax.psum_scatter(grad_outer_weight.astype(jnp.bfloat16), 'fsdp', scatter_...  48.4 us
    unnamed x2, blocking collectives  24.4 us
    psum x1, blocking collectives, local(): lax.psum(shards[1].astype(jnp.bfloat16), 'dp').astype(jnp.float32)  21.7 us
    dot_general x2, matrix products, forward(): jnp.dot(active, outer_weight, preferred_element_type=jnp.float32)  19.1 us
    dot_general x1, matrix products, local(): jnp.dot(grad_outer_low, full_outer.T, preferred_element_type=jnp.float32)  18.2 us
  transfers between devices with their start and end apart: 11, of which 6 were waited for; matrix products, arithmetic and copies ran while one was open for 48% of the time, Pallas kernels for 0%

commit v1 on v0

--- a/solution.py
+++ b/solution.py
@@ -1,29 +1,524 @@
+import functools
 from functools import partial
 
 import jax
 import jax.numpy as jnp
 from jax import lax
+from jax.experimental import pallas as pl
+from jax.experimental.pallas import tpu as pltpu
 from jax.sharding import PartitionSpec as P
 
-D = 768
-HEADS = 12
-HEAD = 64
-TABLE = 768
-SEQ = 512
-
-
-norm_eps = 1e-05
-
-
-def norm_rows(hidden, gain, shift):
+
+SEQ, HEAD, HEADS, D, TABLE = 512, 64, 12, 768, 768
+EPS = 1e-5
+LOG2E = 1.4426950408889634
+F32, BF16 = jnp.float32, jnp.bfloat16
+
+def mm(a, b):
+    return lax.dot_general(a, b, (((1,), (0,)), ((), ())), preferred_element_type=F32)
+
+def mm_nt(a, b):
+    return lax.dot_general(a, b, (((1,), (1,)), ((), ())), preferred_element_type=F32)
+
+def upper_tail(size):
+    t = pl.reciprocal(1.0 + (0.3275911 * 0.7071067811865476) * size, approx=True)
+    bell = jnp.exp2(size * size * (-0.5 * LOG2E))
+    poly = t * (0.127414796 + t * (-0.142248368 + t * (0.7107068705 + t * (-0.7265760135 + t * 0.5307027145))))
+    return poly * bell, bell
+
+def norm_parts(hidden):
     center = jnp.mean(hidden, axis=-1, keepdims=True)
     offset = hidden - center
     spread = jnp.mean(offset * offset, axis=-1, keepdims=True)
-    return offset * lax.rsqrt(spread + norm_eps) * gain + shift
-
-
-def norm_back(hidden, gain, shift, incoming):
-    _, pull = jax.vjp(norm_rows, hidden, gain.astype(jnp.float32), shift.astype(jnp.float32))
+    inv = lax.rsqrt(spread + EPS)
+    return offset * inv, inv
+
+def row_of(vec_ref, k):
+    n = vec_ref.shape[0]
+    total = vec_ref[0, k:k + 1, :].astype(F32)
+    for s in range(1, n):
+        total = total + vec_ref[s, k:k + 1, :].astype(F32)
+    return total
+
+def embed_rows(ids_ref, tokens_ref, tab_ref, start_ref):
+    lanes = lax.broadcasted_iota(jnp.int32, (128, 128), 1).astype(F32)
+    def step(i, _):
+        ids = jnp.broadcast_to(ids_ref[pl.ds(i, 1), :], (128, 128)).T
+        hot = jnp.concatenate([(ids == lanes + 128.0 * j).astype(F32).astype(BF16) for j in range(TABLE // 128)], axis=1)
+        rows = pl.ds(pl.multiple_of(i * 128, 128), 128)
+        emb = mm(hot, tab_ref[...])
+        kept = jnp.concatenate([ids] * (D // 128), axis=1) < 0.0
+        start_ref[rows, :] = jnp.where(kept, tokens_ref[rows, :].astype(F32), emb).astype(BF16)
+        return 0
+    lax.fori_loop(0, ids_ref.shape[0], step, 0)
+
+def make_colbias(vec_ref, colb_ref):
+    for part, k in ((0, 1), (1, None), (2, 2)):
+        row = None if k is None else row_of(vec_ref, k)
+        for j in range(D // 128):
+            tile = jnp.zeros((128, 128), F32) if k is None else jnp.broadcast_to(row[:, 128 * j:128 * j + 128], (128, 128)).T
+            colb_ref[part * D + 128 * j:part * D + 128 * j + 128, :] = tile
+
+def qkv_rows(o, size, wt_ref, start_ref, colb_ref, qkvt_ref):
+    rows = pl.ds(pl.multiple_of(o, 64), size)
+    tokens = start_ref.shape[0]
+    acc = mm_nt(wt_ref[rows, :], start_ref[...])
+    bias = jnp.concatenate([colb_ref[rows, :]] * (tokens // 128), axis=1)
+    qkvt_ref[rows, :] = (acc + bias).astype(BF16)
+
+def attend_pair(page, pair, qkvt_ref, att_ref):
+    cols = pl.ds(pl.multiple_of(page * SEQ, SEQ), SEQ)
+    ones = jnp.ones((16, SEQ), BF16)
+    outs = []
+    for sub in range(2):
+        head = pair * 2 + sub
+        at = lambda part: pl.ds(pl.multiple_of(part * D + head * HEAD, HEAD), HEAD)
+        qt = qkvt_ref[at(0), cols]
+        kn = qkvt_ref[at(1), cols].T
+        vt = jnp.concatenate([qkvt_ref[at(2), cols], ones], axis=0)
+        halves = []
+        for c in range(2):
+            s = mm(kn, qt[:, 256 * c:256 * c + 256])
+            top = jnp.max(s, axis=0, keepdims=True)
+            e = jnp.exp2((s - top) * (LOG2E * HEAD ** -0.5)).astype(BF16)
+            o = mm(vt, e)
+            halves.append(o[:HEAD] / o[HEAD:HEAD + 1])
+        outs.append(jnp.concatenate(halves, axis=1))
+    both = jnp.concatenate(outs, axis=0)
+    att_ref[cols, pl.ds(pl.multiple_of(pair * 128, 128), 128)] = both.T.astype(BF16)
+
+def proj_norm(i, size, att_ref, wpt_ref, start_ref, vec_ref, first_ref, low_ref):
+    rows = pl.ds(pl.multiple_of(i * size, size), size)
+    h = start_ref[rows, :].astype(F32) + (mm_nt(att_ref[rows, :], wpt_ref[...]) + row_of(vec_ref, 3))
+    xhat, _ = norm_parts(h)
+    first = xhat * row_of(vec_ref, 4) + row_of(vec_ref, 5)
+    low_ref[rows, :] = first.astype(BF16)
+    first_ref[rows, :] = first + row_of(vec_ref, 6)
+
+def ff_part(s, i, size, low_ref, w1_ref, w2_ref, vec_ref, acc_ref):
+    rows = pl.ds(pl.multiple_of(i * size, size), size)
+    x = mm(low_ref[rows, :], w1_ref[s]) + vec_ref[s, 0:1, :].astype(F32)
+    a = jnp.abs(x)
+    q, _ = upper_tail(a)
+    active = (jnp.maximum(x, 0.0) - a * q).astype(BF16)
+    acc_ref[rows, :] += mm(active, w2_ref[s])
+
+def out_norm(i, size, acc_ref, vec_ref, out_ref):
+    rows = pl.ds(pl.multiple_of(i * size, size), size)
+    xhat, _ = norm_parts(acc_ref[rows, :])
+    out_ref[rows, :] = (xhat * row_of(vec_ref, 7) + row_of(vec_ref, 8)).astype(BF16)
+
+def fwd_kernel(tokens, idf, tab, wt, wpt, w1, w2, vec, out, start, att, qkvt, colb, acc, low):
+    T = tokens.shape[0]
+    pages = T // SEQ
+    make_colbias(vec, colb)
+    embed_rows(idf, tokens, tab, start)
+    @pl.loop(0, 9)
+    def _(o):
+        qkv_rows(o * 256, 256, wt, start, colb, qkvt)
+    @pl.loop(0, pages * 6)
+    def _(it):
+        attend_pair(it // 6, it % 6, qkvt, att)
+    @pl.loop(0, T // 256)
+    def _(i):
+        proj_norm(i, 256, att, wpt, start, vec, acc, low)
+    @pl.loop(0, 4 * (T // 512))
+    def _(it):
+        ff_part(it // (T // 512), it % (T // 512), 512, low, w1, w2, vec, acc)
+    @pl.loop(0, T // 256)
+    def _(i):
+        out_norm(i, 256, acc, vec, out)
+
+def forward_call(tokens, idf, tab, wt, wpt, w1, w2, vec):
+    T = tokens.shape[0]
+    vm = pl.BlockSpec(memory_space=pltpu.VMEM)
+    return pl.pallas_call(
+        fwd_kernel,
+        out_shape=[jax.ShapeDtypeStruct((T, D), BF16), jax.ShapeDtypeStruct((T, D), BF16), jax.ShapeDtypeStruct((T, D), BF16), jax.ShapeDtypeStruct((3 * D, T), BF16)],
+        in_specs=[vm] * 8, out_specs=[vm] * 4,
+        scratch_shapes=[pltpu.VMEM((3 * D, 128), F32), pltpu.VMEM((T, D), F32), pltpu.VMEM((T, D), BF16)],
+        compiler_params=pltpu.CompilerParams(vmem_limit_bytes=60 * 2**20), name="forward",
+    )(tokens, idf, tab, wt, wpt, w1, w2, vec)
+
+
+ROWS_OUTER, ROWS_INNER, ROWS_PROJ, ROWS_QKV, ROWS_TABLE, ROWS_VEC = 0, 768, 1536, 1728, 2304, 2496
+ROWS = 2560
+HALF = 128
+
+def mm_tn(a, b):
+    return mm(a.T, b)
+
+def norm_back(xhat, inv, gain, g):
+    gx = g * gain
+    return inv * (gx - jnp.mean(gx, axis=-1, keepdims=True) - xhat * jnp.mean(gx * xhat, axis=-1, keepdims=True))
+
+def put(ref, index, value, first):
+    if first:
+        ref[index] = value.astype(ref.dtype)
+    else:
+        ref[index] = (ref[index].astype(F32) + value).astype(ref.dtype)
+
+def bwd_kernel(nb_ref, idf, start_h, att_h, cot_h, qkvt_h, wt_h, wpt_h, w1_h, w2_h, vec_h, grad_h, token_h,
+               start, att, cot, qkvt, wpt, w1, w2, vec, grad, tok,
+               active, slope, low, acc, xhat_one, g_first, qct, gact, gone, gqc, gkv, gall, sums, pick, rank, sem_in, sem_out):
+    T = start.shape[0]
+    pages = T // SEQ
+    W = pages * HALF
+    arrivals = {}
+    for k, (name, src, dst) in enumerate((("vec", vec_h, vec), ("start", start_h, start), ("att", att_h, att), ("wpt", wpt_h, wpt), ("w1", w1_h, w1), ("w2", w2_h, w2),
+                                          ("cot", cot_h, cot), ("qkvt", qkvt_h, qkvt))):
+        arrivals[name] = pltpu.make_async_copy(src, dst, sem_in.at[k])
+        arrivals[name].start()
+
+    r_i = lax.broadcasted_iota(jnp.int32, (SEQ, SEQ), 0)
+    c_i = lax.broadcasted_iota(jnp.int32, (SEQ, SEQ), 1)
+    upper = (r_i < c_i).astype(F32).astype(BF16)
+    per = SEQ // 128
+    for p in range(pages):
+        ids = jnp.concatenate([idf[per * p + k:per * p + k + 1, :] for k in range(per)], axis=1)
+        ids8 = jnp.broadcast_to(ids, (8, SEQ))
+        hit = (ids8 >= 0.0).astype(F32)
+        before = mm(jnp.concatenate([hit, hit], axis=0).astype(BF16), upper)[:8]
+        rank[p] = jnp.where(ids8 >= 0.0, before, -1e6)
+
+    sums[...] = jnp.zeros_like(sums)
+    row_j = lax.broadcasted_iota(jnp.int32, (HALF, SEQ), 0).astype(F32)
+
+    def make_pick(b):
+        for p in range(pages):
+            want = row_j + (b * HALF).astype(F32) if not isinstance(b, int) else row_j + float(b * HALF)
+            pick[p] = (jnp.broadcast_to(rank[p][0:1, :], (HALF, SEQ)) == want).astype(F32).astype(BF16)
+
+    def picked(ref):
+        return jnp.concatenate([mm(pick[p], ref[p * SEQ:(p + 1) * SEQ, :]) for p in range(pages)], axis=0)
+
+    def block(b, first):
+        wait = (lambda n: arrivals[n].wait()) if first else (lambda n: None)
+        make_pick(b)
+        wait("start"); wait("att"); wait("vec"); wait("wpt")
+        start_c = picked(start)
+        att_c = picked(att).astype(BF16)
+        h = start_c + (mm_nt(att_c, wpt[...]) + row_of(vec, 3))
+        xhat, inv_one = norm_parts(h)
+        xhat_one[...] = xhat
+        f = xhat * row_of(vec, 4) + row_of(vec, 5)
+        low[...] = f.astype(BF16)
+        acc[...] = f + row_of(vec, 6)
+        wait("w1"); wait("w2")
+        @pl.loop(0, 4)
+        def _(s):
+            x = mm(low[...], w1[s]) + vec[s, 0:1, :].astype(F32)
+            a = jnp.abs(x)
+            q, bell = upper_tail(a)
+            active[s] = (jnp.maximum(x, 0.0) - a * q).astype(BF16)
+            slope[s] = (jnp.where(x >= 0.0, 1.0 - q, q) + x * (bell * 0.3989422804014327)).astype(BF16)
+            acc[...] += mm(active[s], w2[s])
+        xhat_two, inv_two = norm_parts(acc[...])
+        wait("cot")
+        g_out = picked(cot)
+        sums[9:10, :] += jnp.sum(g_out * xhat_two, axis=0, keepdims=True)
+        sums[10:11, :] += jnp.sum(g_out, axis=0, keepdims=True)
+        g_two = norm_back(xhat_two, inv_two, row_of(vec, 7), g_out)
+        g_outer = g_two.astype(BF16)
+        sums[8:9, :] += jnp.sum(g_outer.astype(F32), axis=0, keepdims=True)
+        g_first[...] = g_two
+        low_t = low[...].T
+        @pl.loop(0, 4)
+        def _(s):
+            put(grad, (s, pl.ds(ROWS_OUTER, D)), mm_tn(active[s], g_outer), first)
+            g_inner = (mm_nt(g_outer, w2[s]) * slope[s].astype(F32)).astype(BF16)
+            sums[pl.ds(s, 1), :] += jnp.sum(g_inner.astype(F32), axis=0, keepdims=True)
+            put(grad, (s, pl.ds(ROWS_INNER, D)), mm(low_t, g_inner), first)
+            g_first[...] += mm_nt(g_inner, w1[s])
+        g = g_first[...]
+        xhat = xhat_one[...]
+        sums[6:7, :] += jnp.sum(g * xhat, axis=0, keepdims=True)
+        sums[7:8, :] += jnp.sum(g, axis=0, keepdims=True)
+        g_one = norm_back(xhat, inv_one, row_of(vec, 4), g)
+        gone[b] = g_one
+        g_proj = g_one.astype(BF16)
+        sums[5:6, :] += jnp.sum(g_proj.astype(F32), axis=0, keepdims=True)
+        dwp = mm_tn(g_proj, att_c)
+        for s in range(4):
+            put(grad, (s, pl.ds(ROWS_PROJ, 192)), dwp[192 * s:192 * s + 192], first)
+        gact[...] = mm(g_proj, wpt[...]).astype(BF16).T
+        wait("qkvt")
+        for p in range(pages):
+            qct[:, p * HALF:(p + 1) * HALF] = mm_nt(qkvt[0:D, p * SEQ:(p + 1) * SEQ], pick[p]).astype(BF16)
+        @pl.loop(0, pages * 6)
+        def _(it):
+            page, pair = it // 6, it % 6
+            cols = pl.ds(pl.multiple_of(page * SEQ, SEQ), SEQ)
+            small = pl.ds(pl.multiple_of(page * HALF, HALF), HALF)
+            for sub in range(2):
+                head = pair * 2 + sub
+                at = lambda part: pl.ds(pl.multiple_of(part * D + head * HEAD, HEAD), HEAD)
+                kt = qkvt[at(1), cols]
+                vn = qkvt[at(2), cols].T
+                qt = qct[at(0), small]
+                ga = gact[at(0), small]
+                s = mm(kt.T, qt)
+                top = jnp.max(s, axis=0, keepdims=True)
+                e = jnp.exp2((s - top) * (LOG2E * HEAD ** -0.5))
+                p = e * (1.0 / jnp.sum(e, axis=0, keepdims=True))
+                gp = mm(vn, ga)
+                d = jnp.sum(p * gp, axis=0, keepdims=True)
+                gs = (p * (gp - d) * HEAD ** -0.5).astype(BF16)
+                gqc[b, at(0), small] = mm(kt, gs).astype(BF16)
+                put(gkv, (at(0), cols), mm_nt(qt, gs), first)
+                put(gkv, (at(1), cols), mm_nt(ga, p.astype(BF16)), first)
+        dwq = mm(gqc[b], start_c.astype(BF16))
+        put(grad, (0, pl.ds(ROWS_QKV, 576)), dwq[:576], first)
+        put(grad, (1, pl.ds(ROWS_QKV, 192)), dwq[576:], first)
+        ones = jnp.ones((16, W), BF16)
+        sums[4:5, :] += mm_nt(ones, gqc[b])[0:1]
+
+    def table_block(b, first):
+        make_pick(b)
+        gall[0:D, :] = gqc[b]
+        hots = []
+        for p in range(pages):
+            gall[D:3 * D, p * HALF:(p + 1) * HALF] = mm_nt(gkv[:, p * SEQ:(p + 1) * SEQ], pick[p]).astype(BF16)
+            ids = jnp.concatenate([idf[per * p + k:per * p + k + 1, :] for k in range(per)], axis=1)
+            hot = (jnp.broadcast_to(ids, (TABLE, SEQ)) == lax.broadcasted_iota(jnp.int32, (TABLE, SEQ), 0).astype(F32)).astype(F32).astype(BF16)
+            hots.append(mm_nt(hot, pick[p]).astype(BF16))
+        gt = gall[...].T
+        g_start = gone[b] + sum(mm(gt[:, D * k:D * k + D], w2[k]) for k in range(3))
+        dtab = mm(jnp.concatenate(hots, axis=1), g_start.astype(BF16))
+        for s in range(4):
+            put(grad, (s, pl.ds(ROWS_TABLE, 192)), dtab[192 * s:192 * s + 192], first)
+
+    nb = nb_ref[0]
+    block(0, True)
+    @pl.loop(1, nb)
+    def _(b):
+        block(b, False)
+    outs = []
+    def send(k, src, dst):
+        c = pltpu.make_async_copy(src, dst, sem_out.at[k]); c.start(); outs.append(c)
+    for s in range(4):
+        send(s, grad.at[s, pl.ds(0, ROWS_QKV)], grad_h.at[s, pl.ds(0, ROWS_QKV)])
+    wt_copy = pltpu.make_async_copy(wt_h, w2.at[pl.ds(0, 3)], sem_in.at[8])
+    wt_copy.start()
+    @pl.loop(0, 8)
+    def _(i):
+        o = 192 * i
+        at = D + o
+        grad[at // 576, pl.ds(pl.multiple_of(ROWS_QKV + at % 576, 64), 192)] = mm(gkv[pl.ds(pl.multiple_of(o, 64), 192), :], start[...]).astype(BF16)
+    sums[11:12, :] += mm_nt(jnp.ones((16, T), BF16), gkv[D:2 * D, :])[0:1]
+    wt_copy.wait()
+    table_block(0, True)
+    @pl.loop(1, nb)
+    def _(b):
+        table_block(b, False)
+    for s in range(4):
+        rest = jnp.concatenate([sums[4:12, :], jnp.zeros((7, D), F32)], axis=0)
+        grad[s, ROWS_VEC:ROWS_VEC + 16, :] = jnp.concatenate([sums[s:s + 1, :], rest], axis=0).astype(BF16)
+        grad[s, ROWS_VEC + 16:ROWS, :] = jnp.zeros((ROWS - ROWS_VEC - 16, D), BF16)
+        send(4 + s, grad.at[s, pl.ds(ROWS_QKV, ROWS - ROWS_QKV)], grad_h.at[s, pl.ds(ROWS_QKV, ROWS - ROWS_QKV)])
+    @pl.loop(0, T // 256)
+    def _(i):
+        rows = pl.ds(pl.multiple_of(i * 256, 256), 256)
+        gt = gkv[:, rows].T
+        g = mm(gt[:, :D], w2[1]) + mm(gt[:, D:], w2[2])
+        slot = i % 2
+        @pl.when(i >= 2)
+        def _():
+            pltpu.make_async_copy(tok.at[slot], token_h.at[pl.ds(pl.multiple_of(i * 256 - 512, 256), 256)], sem_out.at[8 + slot]).wait()
+        for k in range(2):
+            ids = jnp.broadcast_to(idf[pl.ds(2 * i + k, 1), :], (128, 128)).T
+            kept = jnp.concatenate([ids] * (D // 128), axis=1) < 0.0
+            tok[slot, 128 * k:128 * k + 128, :] = jnp.where(kept, g[128 * k:128 * k + 128], 0.0)
+        pltpu.make_async_copy(tok.at[slot], token_h.at[rows], sem_out.at[8 + slot]).start()
+    for c in outs: c.wait()
+    for i in range(T // 256 - 2, T // 256):
+        pltpu.make_async_copy(tok.at[i % 2], token_h.at[pl.ds(256 * i, 256)], sem_out.at[8 + i % 2]).wait()
+
+def backward_call(nb, idf, start, att, cot, qkvt, wt, wpt, w1, w2, vec):
+    T = start.shape[0]
+    pages = T // SEQ
+    W = pages * HALF
+    n = w1.shape[0]
+    top = SEQ // HALF
+    vm = pl.BlockSpec(memory_space=pltpu.VMEM)
+    hb = pl.BlockSpec(memory_space=pl.ANY)
+    same = lambda a: pltpu.VMEM(a.shape, a.dtype)
+    return pl.pallas_call(
+        bwd_kernel,
+        out_shape=[jax.ShapeDtypeStruct((n, ROWS, D), BF16), jax.ShapeDtypeStruct((T, D), F32)],
+        in_specs=[pl.BlockSpec(memory_space=pltpu.SMEM), vm] + [hb] * 9, out_specs=[hb] * 2,
+        scratch_shapes=[same(a) for a in (start, att, cot, qkvt, wpt, w1, w2, vec)] + [
+            pltpu.VMEM((n, ROWS, D), BF16), pltpu.VMEM((2, 256, D), F32),
+            pltpu.VMEM((n, W, D), BF16), pltpu.VMEM((n, W, D), BF16), pltpu.VMEM((W, D), BF16), pltpu.VMEM((W, D), F32), pltpu.VMEM((W, D), F32), pltpu.VMEM((W, D), F32),
+            pltpu.VMEM((D, W), BF16), pltpu.VMEM((D, W), BF16), pltpu.VMEM((top, W, D), F32), pltpu.VMEM((top, D, W), BF16),
+            pltpu.VMEM((2 * D, T), BF16), pltpu.VMEM((3 * D, W), BF16), pltpu.VMEM((16, D), F32), pltpu.VMEM((pages, HALF, SEQ), BF16), pltpu.VMEM((pages, 8, SEQ), F32),
+            pltpu.SemaphoreType.DMA((9,)), pltpu.SemaphoreType.DMA((10,))],
+        compiler_params=pltpu.CompilerParams(vmem_limit_bytes=62 * 2**20), name="backward",
+    )(nb, idf, start, att, cot, qkvt, wt.reshape(3, D, D), wpt, w1, w2, vec)
+
+
+MESH = pl.DeviceIdType.MESH
+CHUNK = 64
+LAGS = (0, 2, 4, 6, 8, 10, 12)
+
+def reduce_kernel(grad, fin_h, own, rc, sy, ry, kx, sx, rx, kz, sz, rz, se, re, fin, send_sem, recv_sem, own_sem, out_sem):
+    dp, fs = lax.axis_index("dp"), lax.axis_index("fsdp")
+    y, c = fs // 2, fs % 2
+    x, za, zb = dp % 2, (dp // 2) % 2, dp // 4
+    to_c = (dp, 2 * y + 1 - c)
+    to_y = (dp, 2 * (1 - y) + c)
+    to_x = (dp + 1 - 2 * x, fs)
+    to_a = (dp + 2 - 4 * za, fs)
+    to_b = (dp + 4 - 8 * zb, fs)
+    barrier = pltpu.get_barrier_semaphore()
+    for to in (to_c, to_y, to_x, to_a, to_b):
+        pl.semaphore_signal(barrier, inc=1, device_id=to, device_id_type=MESH)
+    pl.semaphore_wait(barrier, 5)
+    n = own.shape[1] // CHUNK
+    H, Q = CHUNK // 2, CHUNK // 4
+    rows = lambda k: pl.ds(pl.multiple_of(k * CHUNK, CHUNK), CHUNK)
+    half = lambda k, s: pl.ds(pl.multiple_of(k * CHUNK + s * H, H), H)
+    quarter = lambda k, s, t: pl.ds(pl.multiple_of(k * CHUNK + s * H + t * Q, Q), Q)
+    hrows = lambda k: pl.ds(pl.multiple_of(k * H, H), H)
+    qrows = lambda k: pl.ds(pl.multiple_of(k * Q, Q), Q)
+    f = lambda v: v.astype(F32)
+
+    def remote(stage, k, src, dst, to):
+        return pltpu.make_async_remote_copy(src_ref=src, dst_ref=dst, send_sem=send_sem.at[stage, k], recv_sem=recv_sem.at[stage, k], device_id=to, device_id_type=MESH)
+    copies = [
+        lambda k: remote(0, k, grad.at[:, 1 - c, rows(k), :], rc.at[:, rows(k), :], to_c),
+        lambda k: remote(1, k, sy.at[rows(k)], ry.at[rows(k)], to_y),
+        lambda k: remote(2, k, sx.at[hrows(k)], rx.at[hrows(k)], to_x),
+        lambda k: remote(3, k, sz.at[qrows(k)], rz.at[qrows(k)], to_a),
+        lambda k: remote(4, k, se.at[qrows(k)], re.at[qrows(k)], to_b),
+        lambda k: remote(5, k, fin.at[quarter(k, x, za)], fin.at[quarter(k, x, za)], to_a),
+        lambda k: remote(6, k, fin.at[half(k, x)], fin.at[half(k, x)], to_x),
+    ]
+    local = lambda k: pltpu.make_async_copy(grad.at[:, c, rows(k), :], own.at[:, rows(k), :], own_sem.at[k])
+    leave = lambda k: pltpu.make_async_copy(fin.at[rows(k)], fin_h.at[rows(k)], out_sem.at[k])
+
+    @pl.loop(0, n)
+    def _(k):
+        copies[0](k).start()
+        local(k).start()
+
+    def on_y(k):
+        copies[0](k).wait_recv()
+        local(k).wait()
+        sy[rows(k), :] = (f(own[1 - y, rows(k), :]) + f(rc[1 - y, rows(k), :])).astype(BF16)
+        copies[1](k).start()
+
+    def on_x(k):
+        copies[1](k).wait_recv()
+        part = lambda s: f(own[y, half(k, s), :]) + f(rc[y, half(k, s), :]) + f(ry[half(k, s), :])
+        sx[hrows(k), :] = part(1 - x).astype(BF16)
+        copies[2](k).start()
+        kx[hrows(k), :] = part(x)
+
+    def on_a(k):
+        copies[2](k).wait_recv()
+        part = lambda t: kx[pl.ds(pl.multiple_of(k * H + t * Q, Q), Q), :] + f(rx[pl.ds(pl.multiple_of(k * H + t * Q, Q), Q), :])
+        sz[qrows(k), :] = part(1 - za).astype(BF16)
+        copies[3](k).start()
+        kz[qrows(k), :] = part(za)
+
+    def on_b(k):
+        copies[3](k).wait_recv()
+        se[qrows(k), :] = (kz[qrows(k), :] + f(rz[qrows(k), :])).astype(BF16)
+        copies[4](k).start()
+
+    def back_a(k):
+        copies[4](k).wait_recv()
+        fin[quarter(k, x, za), :] = (f(se[qrows(k), :]) + f(re[qrows(k), :])).astype(BF16)
+        copies[5](k).start()
+
+    def back_x(k):
+        copies[5](k).wait_recv()
+        copies[6](k).start()
+
+    def done(k):
+        copies[6](k).wait_recv()
+        leave(k).start()
+
+    @pl.loop(0, n + LAGS[-1])
+    def _(t):
+        for stage, lag in zip((on_y, on_x, on_a, on_b, back_a, back_x, done), LAGS):
+            k = t - lag
+            @pl.when((k >= 0) & (k < n))
+            def _():
+                stage(k)
+
+    @pl.loop(0, n)
+    def _(k):
+        for copy in copies:
+            copy(k).wait_send()
+        leave(k).wait()
+
+def reduce_call(grad):
+    R = grad.shape[1]
+    n = R // CHUNK
+    hb = pl.BlockSpec(memory_space=pl.ANY)
+    low = lambda *s: pltpu.VMEM(s + (D,), BF16)
+    return pl.pallas_call(
+        reduce_kernel,
+        out_shape=jax.ShapeDtypeStruct((R, D), BF16),
+        in_specs=[hb], out_specs=hb,
+        scratch_shapes=[low(2, R), low(2, R), low(R), low(R), pltpu.VMEM((R // 2, D), F32), low(R // 2), low(R // 2),
+                        pltpu.VMEM((R // 4, D), F32), low(R // 4), low(R // 4), low(R // 4), low(R // 4), low(R),
+                        pltpu.SemaphoreType.DMA((7, n)), pltpu.SemaphoreType.DMA((7, n)), pltpu.SemaphoreType.DMA((n,)), pltpu.SemaphoreType.DMA((n,))],
+        compiler_params=pltpu.CompilerParams(collective_id=1, has_side_effects=True, vmem_limit_bytes=60 * 2**20), name="reduce",
+    )(grad.reshape(2, 2, R, D))
+
+def finish_kernel(fin, outer, inner, qkv, proj, table, inner_b, *smalls):
+    outer[...] = fin[ROWS_OUTER:ROWS_INNER].astype(F32)
+    inner[...] = fin[ROWS_INNER:ROWS_PROJ].astype(F32)
+    table[...] = fin[ROWS_TABLE:ROWS_VEC].astype(F32)
+    proj[...] = fin[ROWS_PROJ:ROWS_QKV].astype(F32).T
+    qkv[...] = fin[ROWS_QKV:ROWS_TABLE].astype(F32).T
+    rows = fin[ROWS_VEC:ROWS_VEC + 16].astype(F32)
+    inner_b[...] = rows[0]
+    me = lax.axis_index("fsdp")
+    part = D // lax.axis_size("fsdp")
+    for k, ref in enumerate(smalls):
+        ref[...] = sum(jnp.where(me == s, rows[1 + k, part * s:part * s + part], 0.0) for s in range(D // part))
+
+def finish_call(fin):
+    vm = pl.BlockSpec(memory_space=pltpu.VMEM)
+    part = D // lax.axis_size("fsdp")
+    shp = lambda *s: jax.ShapeDtypeStruct(s, F32)
+    out = pl.pallas_call(
+        finish_kernel, out_shape=[shp(D, D), shp(D, D), shp(D, 3 * part), shp(D, part), shp(part, D), shp(D)] + [shp(part)] * 8,
+        in_specs=[vm], out_specs=[vm] * 14, compiler_params=pltpu.CompilerParams(vmem_limit_bytes=40 * 2**20), name="finish")(fin)
+    return *out[:6], out[6:]
+
+def local_direct(tokens, masked_rows, replace_ids, cotangent, qkv_weight, query_bias, value_bias, proj_weight, proj_bias, first_gain, first_shift,
+                 inner_weight, inner_bias, outer_weight, outer_bias, second_gain, second_shift, embed_table):
+    n, me = lax.axis_size("fsdp"), lax.axis_index("fsdp")
+    gather = lambda v: lax.all_gather(v, "fsdp", axis=0, tiled=True)
+    mine = jnp.arange(D) // (D // n) == me
+    place = lambda v: jnp.where(mine, jnp.tile(v, n), 0).astype(BF16)
+    smalls = (query_bias, value_bias, proj_bias, first_gain, first_shift, outer_bias, second_gain, second_shift)
+    vec = jnp.stack([inner_bias] + [place(v) for v in smalls] + [jnp.zeros(D, BF16)] * 7)
+    tab, wt, wpt = gather(embed_table), gather(qkv_weight.T), gather(proj_weight.T)
+    w1, w2, vec = gather(inner_weight[None]), gather(outer_weight[None]), gather(vec[None])
+    idf = jnp.where(masked_rows > 0, replace_ids, -1).astype(F32).reshape(-1, 128)
+    out, start, att, qkvt = forward_call(tokens, idf, tab, wt, wpt, w1, w2, vec)
+    blocks = jnp.max((jnp.sum(masked_rows.reshape(-1, SEQ), axis=1) + HALF - 1) // HALF)[None]
+    grad, token_grad = backward_call(blocks, idf, start, att, cotangent, qkvt, wt, wpt, w1, w2, vec)
+    outer, inner, qkv, proj, table, inner_b, smalls = finish_call(reduce_call(grad))
+    q, pb, fg, fs, ob, sg, ss, v = smalls
+    return (out, token_grad, qkv, q, v, proj, pb, fg, fs, inner, inner_b, outer, ob, sg, ss, table)
+
+
+def plain_norm_rows(hidden, gain, shift):
+    center = jnp.mean(hidden, axis=-1, keepdims=True)
+    offset = hidden - center
+    spread = jnp.mean(offset * offset, axis=-1, keepdims=True)
+    return offset * lax.rsqrt(spread + EPS) * gain + shift
+
+
+def plain_norm_back(hidden, gain, shift, incoming):
+    _, pull = jax.vjp(plain_norm_rows, hidden, gain.astype(jnp.float32), shift.astype(jnp.float32))
     return pull(incoming)
 
 
@@ -64,7 +559,7 @@
     return stacked.reshape(page_qkv.shape[0], 3 * D)
 
 
-def forward(weights, tokens, chosen, onehot):
+def plain_forward(weights, tokens, chosen, onehot):
     (
         qkv_weight,
         query_bias,
@@ -97,7 +592,7 @@
         attended, proj_weight, preferred_element_type=jnp.float32
     ) + proj_bias.astype(jnp.float32)
     hidden_one = start + projected
-    first = norm_rows(hidden_one, first_gain.astype(jnp.float32), first_shift.astype(jnp.float32))
+    first = plain_norm_rows(hidden_one, first_gain.astype(jnp.float32), first_shift.astype(jnp.float32))
     first_low = first.astype(jnp.bfloat16)
     inner = jnp.dot(
         first_low, inner_weight, preferred_element_type=jnp.float32
@@ -110,7 +605,7 @@
     return (start_low, qkv_low, logsum, attended, hidden_one, first_low, inner, active, hidden_two)
 
 
-def local(
+def local_plain(
     tokens,
     masked_rows,
     replace_ids,
@@ -150,8 +645,8 @@
     onehot = (replace_ids[:, None] == jnp.arange(TABLE, dtype=jnp.int32)[None, :]).astype(
         jnp.bfloat16
     )
-    saved = forward(weights, tokens, chosen, onehot)
-    layer_out = norm_rows(
+    saved = plain_forward(weights, tokens, chosen, onehot)
+    layer_out = plain_norm_rows(
         saved[8], weights[11].astype(jnp.float32), weights[12].astype(jnp.float32)
     ).astype(jnp.bfloat16)
     back_weights = (
@@ -170,7 +665,7 @@
         lax.all_gather(second_shift, "fsdp", axis=0, tiled=True),
         lax.all_gather(embed_table, "fsdp", axis=0, tiled=True),
     )
-    saved = forward(back_weights, tokens, chosen, onehot)
+    saved = plain_forward(back_weights, tokens, chosen, onehot)
     start_low, qkv_low, logsum, attended, hidden_one, first_low, inner, active, hidden_two = saved
     (
         full_qkv,
@@ -189,7 +684,7 @@
         full_table,
     ) = back_weights
     grad_out = jnp.where(chosen, cotangent.astype(jnp.float32), 0.0)
-    grad_two, grad_second_gain, grad_second_shift = norm_back(
+    grad_two, grad_second_gain, grad_second_shift = plain_norm_back(
         hidden_two, full_second_gain, full_second_shift, grad_out
     )
     grad_outer_low = grad_two.astype(jnp.bfloat16)
@@ -203,7 +698,7 @@
     grad_first = grad_two + jnp.dot(
         grad_inner_low, full_inner.T, preferred_element_type=jnp.float32
     )
-    grad_one, grad_first_gain, grad_first_shift = norm_back(
+    grad_one, grad_first_gain, grad_first_shift = plain_norm_back(
         hidden_one, full_first_gain, full_first_shift, grad_first
     )
     grad_proj_low = grad_one.astype(jnp.bfloat16)
@@ -309,8 +804,9 @@
 
 
 def solution(mesh):
+    direct = mesh.shape["dp"] == 8 and mesh.shape["fsdp"] == 4
     return jax.shard_map(
-        local,
+        local_direct if direct else local_plain,
         mesh=mesh,
         in_specs=(
             P(("dp", "fsdp"), None),

time: 627 us -> 397 us (0.63); the launches traced: 618 us -> 397 us
  matrix products: 251 us -> 0 us
  Pallas kernels: 0 us -> 226 us
  local copies, waits for them, and re-layouts: 70.3 us -> 5.76 us
  blocking collectives: 51.3 us -> 6.78 us
  waiting for transfers between devices: 186 us -> 142 us
  other arithmetic: 41 us -> 1.42 us
    dot_general x33 -> x0, matrix products: 237 us -> none  [the longest x2 73.8 us: forward(): jnp.dot(first_low, inner_weight, preferred_element_type=jnp.float32)]
    pallas_call x0 -> x4, Pallas kernels: none -> 226 us  [the longest x1 112 us: reduce_call(): pl.pallas_call(reduce_kernel, out_shape=jax.ShapeDtypeStruct((R, D), BF16...]
    all_gather x5, waiting for transfers between devices: 21.9 us -> 139 us  [local_direct(): gather = lambda v: lax.all_gather(v, 'fsdp', axis=0, tiled=True)]
    reduce_scatter x5 -> x0, waiting for transfers between devices: 98.7 us -> none  [the longest x1 50.2 us: local(): lax.psum_scatter(grad_inner_weight.astype(jnp.bfloat16), 'fsdp', scatter_...]
    psum x1 -> x0, waiting for transfers between devices: 62.6 us -> none  [local(): lax.psum(shards[0].astype(jnp.bfloat16), 'dp').astype(jnp.float32)]
    convert_element_type x25 -> x0, other arithmetic: 24.5 us -> none  [the longest x2 7.08 us: attend_back(): grad_raw = (scale * probs * (grad_prob - center)).astype(jnp.bfloat16)]
    unnamed x2 -> x0, blocking collectives: 24.4 us -> none
    psum x1 -> x0, blocking collectives: 21.7 us -> none  [local(): lax.psum(shards[1].astype(jnp.bfloat16), 'dp').astype(jnp.float32)]
  transfers between devices with their start and end apart: 11 -> 5, of which waited for: 6 -> 5; matrix products, arithmetic and copies ran while one was open for 48% -> 1% of each run, Pallas kernels for 0% -> 0%
where the time goes in v1:
time: 397 us
  Pallas kernels  226 us (57%)
  waiting for transfers between devices  142 us (36%)
  between operations  14 us (4%)
  blocking collectives  6.78 us (2%)
  local copies, waits for them, and re-layouts  5.76 us (1%)
    all_gather x5, waiting for transfers between devices, local_direct(): gather = lambda v: lax.all_gather(v, 'fsdp', axis=0, tiled=True)  139 us
    pallas_call x1, Pallas kernels, reduce_call(): pl.pallas_call(reduce_kernel, out_shape=jax.ShapeDtypeStruct((R, D), BF16...  112 us
    pallas_call x1, Pallas kernels, forward_call(): pl.pallas_call(fwd_kernel, out_shape=[jax.ShapeDtypeStruct((T, D), BF16),...  61.7 us
    pallas_call x1, Pallas kernels, backward_call(): pl.pallas_call(bwd_kernel, out_shape=[jax.ShapeDtypeStruct((n, ROWS, D),...  49 us
  transfers between devices with their start and end apart: 5, of which 5 were waited for; matrix products, arithmetic and copies ran while one was open for 1% of the time, Pallas kernels for 0%

profile of v1, /device:TPU:0, one launch (start us, length us, event | category | flops | bytes accessed | tf_op | source)
XLA Modules:
  0.0 396.5 jit_solution(8126809042615861286)
XLA Ops:
  7.2 0.0 copy-start.4
  7.2 0.0 copy-start.5
  7.2 0.0 copy-start.6
  7.2 0.0 copy-start.7
  7.2 0.0 copy-start.8
  7.2 0.0 copy-start.9
  7.2 0.0 copy-start.10
  7.3 0.0 copy-start.11
  7.3 0.0 copy-start.3
  7.3 0.0 copy-start.1
  7.3 0.0 all-gather.13.cloned.1.call-start
  7.3 0.7 all-gather.13.cloned.1.call-update
  8.0 0.0 copy-start.2
  8.0 0.0 all-gather.9.cloned.1.call-start
  8.1 0.7 all-gather.9.cloned.1.call-update
  8.8 0.0 all-gather.11.cloned.1.call-start
  8.8 0.7 all-gather.11.cloned.1.call-update
  9.5 0.0 all-gather.15.cloned.1.call-start
  9.6 0.5 all-gather.15.cloned.1.call-update
  10.1 0.0 all-gather.17.cloned.1.call-start
  10.1 0.5 all-gather.17.cloned.1.call-update
  10.7 0.0 copy-done.4
  10.7 0.1 tile.33
  10.8 0.0 copy-done.5
  10.8 0.1 tile.35
  10.9 0.0 copy-done.6
  10.9 0.1 tile.37
  11.0 0.0 copy-done.7
  11.0 0.1 tile.39
  11.1 0.0 copy-done.8
  11.1 0.1 tile.81
  11.2 0.0 copy-done.9
  11.2 0.1 tile.83
  11.3 0.0 copy-done.10
  11.3 0.1 tile.85
  11.4 0.0 copy-done.11
  11.4 0.1 tile.87
  11.5 0.0 copy-done.3
  11.5 0.0 copy-done.1
  11.5 0.1 reduce_sum.9
  11.7 0.1 stack.11
  11.8 6.8 %all-gather.2 = bf16[64,768]{1,0:T(8,128)(2,1)} all-gather(bf16[16,768]{1,0:T(8,128)(2,1)S(1)} %stack.11), channel_id=4, replica_groups=mesh['dp'=8,'fsdp'=4] {'fsdp'}, dimensions={0}, use_global_device_ids=true | all-gather | bytes 122880 | tf_op jit(solution)/shard_map/all_gather | solution.py:497
  18.6 0.6 fusion.1
  19.3 0.0 copy-done.2
  19.3 0.6 convert_bitcast_fusion.idf
  19.9 10.0 %all-gather.13.cloned.1.call-done.wpt.wpt_h = bf16[768,768]{1,0:T(8,128)(2,1)} async-done(((bf16[192,768]{1,0:T(8,128)(2,1)}), bf16[768,768]{1,0:T(8,128)(2,1)}) %all-gather.13.cloned.1.call-update) | async-done | bytes 1179664 | tf_op jit(solution)/shard_map/all_gather | solution.py:497
  29.9 19.1 %all-gather.9.cloned.1.call-done.tab = bf16[768,768]{1,0:T(8,128)(2,1)} async-done(((bf16[192,768]{1,0:T(8,128)(2,1)}), bf16[768,768]{1,0:T(8,128)(2,1)}) %all-gather.9.cloned.1.call-update) | async-done | bytes 1179664 | tf_op jit(solution)/shard_map/all_gather | solution.py:497
  48.9 32.4 %all-gather.11.cloned.1.call-done.wt = bf16[2304,768]{1,0:T(8,128)(2,1)} async-done(((bf16[576,768]{1,0:T(8,128)(2,1)}), bf16[2304,768]{1,0:T(8,128)(2,1)}) %all-gather.11.cloned.1.call-update) | async-done | bytes 3538960 | tf_op jit(solution)/shard_map/all_gather | solution.py:497
  81.3 38.9 %all-gather.15.cloned.1.call-done = bf16[3072,768]{1,0:T(8,128)(2,1)} async-done(((bf16[768,768]{1,0:T(8,128)(2,1)}), bf16[3072,768]{1,0:T(8,128)(2,1)}) %all-gather.15.cloned.1.call-update) | async-done | bytes 4718608 | tf_op jit(solution)/shard_map/all_gather | solution.py:497
  120.2 38.9 %all-gather.17.cloned.1.call-done = bf16[3072,768]{1,0:T(8,128)(2,1)} async-done(((bf16[768,768]{1,0:T(8,128)(2,1)}), bf16[3072,768]{1,0:T(8,128)(2,1)}) %all-gather.17.cloned.1.call-update) | async-done | bytes 4718608 | tf_op jit(solution)/shard_map/all_gather | solution.py:497
  159.1 61.7 %forward.1 = (bf16[1024,768]{1,0:T(8,128)(2,1)}, bf16[1024,768]{1,0:T(8,128)(2,1)}, bf16[1024,768]{1,0:T(8,128)(2,1)}, bf16[2304,1024]{1,0:T(8,128)(2,1)}) custom-call(bf16[1024,768]{1,0:T(8,128)(2,1)} %tokens.1, f32[8,128]{1,0:T(8,128)} %convert_bitcast_fusion.idf, bf16[768,768]{1,0:T(8,128)(2,1)} %all-gather.9.cloned.1.call-done.tab, ...), custom_call_target="tpu_custom_call" | custom-call | tf_op jit(solution)/shard_map/forward/pallas_call | solution.py:135
  220.8 49.0 %backward.1 = (bf16[4,2560,768]{2,1,0:T(8,128)(2,1)}, f32[1024,768]{1,0:T(8,128)}) custom-call(s32[1]{0:T(128)} %bitcast.6.nb_ref, f32[8,128]{1,0:T(8,128)} %convert_bitcast_fusion.idf, bf16[1024,768]{1,0:T(8,128)(2,1)} %get-tuple-element.37.start_h, bf16[1024,768]{1,0:T(8,128)(2,1)} %get-tuple-element.38.att_h, bf16[1024,768]{1,0:T(8,128)(2,1)} %cot_h.1, ...), custom_call_target="tpu_custom_call" | custom-call | tf_op jit(solution)/shard_map/backward/pallas_call | solution.py:346
  269.9 112.3 %reduce.1.fin = bf16[2560,768]{1,0:T(8,128)(2,1)} custom-call(bf16[2,2,2560,768]{3,2,1,0:T(8,128)(2,1)} %bitcast.14), custom_call_target="tpu_custom_call" | custom-call | tf_op jit(solution)/shard_map/reduce/pallas_call | solution.py:462
  382.2 0.0 copy-start
  382.2 2.1 copy-done
  384.3 2.9 finish.1
  387.2 1.7 copy.36
  389.0 1.1 copy.37
  (17 shorter events, 0.1 us)
Async XLA Ops:
  7.2 3.5 copy-start.4
  7.2 3.6 copy-start.5
  7.2 3.7 copy-start.6
  7.2 3.8 copy-start.7
  7.2 3.9 copy-start.8
  7.2 3.9 copy-start.9
  7.2 4.0 %copy-start.10 = (bf16[192]{0:T(256)(128)(2,1)S(1)}, bf16[192]{0:T(256)(128)(2,1)}, u32[]{:S(2)}) copy-start(bf16[192]{0:T(256)(128)(2,1)} %param.33) | copy-start | bytes 1156
  7.3 4.1 %copy-start.11 = (bf16[192]{0:T(256)(128)(2,1)S(1)}, bf16[192]{0:T(256)(128)(2,1)}, u32[]{:S(2)}) copy-start(bf16[192]{0:T(256)(128)(2,1)} %param.34) | copy-start | bytes 1156
  7.3 4.2 %copy-start.3 = (bf16[768]{0:T(1024)(128)(2,1)S(1)}, bf16[768]{0:T(1024)(128)(2,1)}, u32[]{:S(2)}) copy-start(bf16[768]{0:T(1024)(128)(2,1)} %param.30) | copy-start | bytes 4612
  7.3 4.2 %copy-start.1 = (s32[1024]{0:T(1024)S(1)}, s32[1024]{0:T(1024)}, u32[]{:S(2)}) copy-start(s32[1024]{0:T(1024)} %param.19) | copy-start | bytes 12292
  7.3 22.6 %all-gather.13.cloned.1.call-start = ((), (), s32[]{:S(2)}) async-start(), calls=%async_computation.2 | async-start | bytes 1474560 | tf_op jit(solution)/shard_map/all_gather | solution.py:497
  8.0 11.2 %copy-start.2 = (s32[1024]{0:T(1024)S(1)}, s32[1024]{0:T(1024)}, u32[]{:S(2)}) copy-start(s32[1024]{0:T(1024)} %param.20) | copy-start | bytes 12292
  8.0 40.9 %all-gather.9.cloned.1.call-start = ((), (), s32[]{:S(2)}) async-start(), calls=%async_computation | async-start | bytes 1474560 | tf_op jit(solution)/shard_map/all_gather | solution.py:497
  8.8 72.5 %all-gather.11.cloned.1.call-start = ((), (), s32[]{:S(2)}) async-start(), calls=%async_computation.1 | async-start | bytes 4423680 | tf_op jit(solution)/shard_map/all_gather | solution.py:497
  9.5 110.7 %all-gather.15.cloned.1.call-start = ((), (), s32[]{:S(2)}) async-start(), calls=%async_computation.3 | async-start | bytes 5898240 | tf_op jit(solution)/shard_map/all_gather | solution.py:497
  10.1 149.0 %all-gather.17.cloned.1.call-start = ((), (), s32[]{:S(2)}) async-start(), calls=%async_computation.4 | async-start | bytes 5898240 | tf_op jit(solution)/shard_map/all_gather | solution.py:497
  382.2 2.1 copy-start
Sparse Core Ops, SparseCore 0:
  9.7 20.1 all-gather.12
  31.4 17.4 all-gather.8
  50.5 30.7 all-gather.10
  82.7 37.4 all-gather.14
  121.6 37.4 all-gather.16

commit v2 on v1

--- a/solution.py
+++ b/solution.py
@@ -13,6 +13,11 @@
 EPS = 1e-5
 LOG2E = 1.4426950408889634
 F32, BF16 = jnp.float32, jnp.bfloat16
+MESH = pl.DeviceIdType.MESH
+
+PART = 192
+TAB, QKV, PROJ, INNER, OUTER, ITEMS = 0, 1, 4, 5, 9, 13
+V_QUERY, V_VALUE, V_PROJ, V_GAIN1, V_SHIFT1, V_OUTER, V_GAIN2, V_SHIFT2 = range(4, 12)
 
 def mm(a, b):
     return lax.dot_general(a, b, (((1,), (0,)), ((), ())), preferred_element_type=F32)
@@ -34,48 +39,67 @@
     return offset * inv, inv
 
 def row_of(vec_ref, k):
-    n = vec_ref.shape[0]
-    total = vec_ref[0, k:k + 1, :].astype(F32)
-    for s in range(1, n):
-        total = total + vec_ref[s, k:k + 1, :].astype(F32)
-    return total
-
-def embed_rows(ids_ref, tokens_ref, tab_ref, start_ref):
+    return vec_ref[k, 0:1, :]
+
+def place_vectors(fs, smalls, parts):
+    for s in range(4):
+        @pl.when(fs == s)
+        def _():
+            inner_bias = smalls[0][...].reshape(1, D)
+            rows = [inner_bias[:, PART * j:PART * j + PART] for j in range(4)] + [v[...].reshape(1, PART) for v in smalls[1:]]
+            rows.append(jnp.zeros((4, PART), BF16))
+            mine = jnp.concatenate(rows, axis=0)
+            sides = [jnp.zeros((16, PART * s), BF16)] * (s > 0) + [mine] + [jnp.zeros((16, D - PART * s - PART), BF16)] * (s < 3)
+            parts[s] = jnp.concatenate(sides, axis=1)
+
+def sum_vectors(parts_ref, vec_ref):
+    total = parts_ref[0].astype(F32)
+    for s in range(1, parts_ref.shape[0]):
+        total = total + parts_ref[s].astype(F32)
+    for k in range(12):
+        vec_ref[k] = jnp.broadcast_to(total[k:k + 1, :], (8, D))
+
+def item(ref, m):
+    return ref[pl.ds(m * D if isinstance(m, int) else pl.multiple_of(m * D, D), D), :]
+
+def embed_rows(idf, tokens, tab, start):
     lanes = lax.broadcasted_iota(jnp.int32, (128, 128), 1).astype(F32)
     def step(i, _):
-        ids = jnp.broadcast_to(ids_ref[pl.ds(i, 1), :], (128, 128)).T
+        ids = jnp.broadcast_to(idf[pl.ds(i, 1), :], (128, 128)).T
         hot = jnp.concatenate([(ids == lanes + 128.0 * j).astype(F32).astype(BF16) for j in range(TABLE // 128)], axis=1)
         rows = pl.ds(pl.multiple_of(i * 128, 128), 128)
-        emb = mm(hot, tab_ref[...])
+        emb = mm(hot, item(tab, TAB))
         kept = jnp.concatenate([ids] * (D // 128), axis=1) < 0.0
-        start_ref[rows, :] = jnp.where(kept, tokens_ref[rows, :].astype(F32), emb).astype(BF16)
+        start[rows, :] = jnp.where(kept, tokens[rows, :].astype(F32), emb).astype(BF16)
         return 0
-    lax.fori_loop(0, ids_ref.shape[0], step, 0)
-
-def make_colbias(vec_ref, colb_ref):
-    for part, k in ((0, 1), (1, None), (2, 2)):
-        row = None if k is None else row_of(vec_ref, k)
+    lax.fori_loop(0, idf.shape[0], step, 0)
+
+def make_colbias(vec, colb):
+    for part, k in ((0, V_QUERY), (1, None), (2, V_VALUE)):
         for j in range(D // 128):
-            tile = jnp.zeros((128, 128), F32) if k is None else jnp.broadcast_to(row[:, 128 * j:128 * j + 128], (128, 128)).T
-            colb_ref[part * D + 128 * j:part * D + 128 * j + 128, :] = tile
-
-def qkv_rows(o, size, wt_ref, start_ref, colb_ref, qkvt_ref):
-    rows = pl.ds(pl.multiple_of(o, 64), size)
-    tokens = start_ref.shape[0]
-    acc = mm_nt(wt_ref[rows, :], start_ref[...])
-    bias = jnp.concatenate([colb_ref[rows, :]] * (tokens // 128), axis=1)
-    qkvt_ref[rows, :] = (acc + bias).astype(BF16)
-
-def attend_pair(page, pair, qkvt_ref, att_ref):
+            tile = jnp.zeros((128, 128), F32) if k is None else jnp.broadcast_to(vec[k, 0:1, 128 * j:128 * j + 128], (128, 128)).T
+            colb[part * D + 128 * j:part * D + 128 * j + 128, :] = tile
+
+def qkv_item(j, all_w, start, colb, qkvt):
+    @pl.loop(0, start.shape[0] // 256)
+    def _(i):
+        cols = pl.ds(pl.multiple_of(i * 256, 256), 256)
+        acc = mm_nt(item(all_w, QKV + j), start[cols, :])
+        for s in range(4):
+            at = 3 * PART * s + PART * j
+            bias = jnp.concatenate([colb[at:at + PART, :]] * 2, axis=1)
+            qkvt[at:at + PART, cols] = (acc[PART * s:PART * s + PART] + bias).astype(BF16)
+
+def attend_pair(page, pair, qkvt, att):
     cols = pl.ds(pl.multiple_of(page * SEQ, SEQ), SEQ)
     ones = jnp.ones((16, SEQ), BF16)
     outs = []
     for sub in range(2):
         head = pair * 2 + sub
         at = lambda part: pl.ds(pl.multiple_of(part * D + head * HEAD, HEAD), HEAD)
-        qt = qkvt_ref[at(0), cols]
-        kn = qkvt_ref[at(1), cols].T
-        vt = jnp.concatenate([qkvt_ref[at(2), cols], ones], axis=0)
+        qt = qkvt[at(0), cols]
+        kn = qkvt[at(1), cols].T
+        vt = jnp.concatenate([qkvt[at(2), cols], ones], axis=0)
         halves = []
         for c in range(2):
             s = mm(kn, qt[:, 256 * c:256 * c + 256])
@@ -85,65 +109,197 @@
             halves.append(o[:HEAD] / o[HEAD:HEAD + 1])
         outs.append(jnp.concatenate(halves, axis=1))
     both = jnp.concatenate(outs, axis=0)
-    att_ref[cols, pl.ds(pl.multiple_of(pair * 128, 128), 128)] = both.T.astype(BF16)
-
-def proj_norm(i, size, att_ref, wpt_ref, start_ref, vec_ref, first_ref, low_ref):
+    att[cols, pl.ds(pl.multiple_of(pair * 128, 128), 128)] = both.T.astype(BF16)
+
+def proj_norm(i, size, att, all_w, start, vec, acc, low):
     rows = pl.ds(pl.multiple_of(i * size, size), size)
-    h = start_ref[rows, :].astype(F32) + (mm_nt(att_ref[rows, :], wpt_ref[...]) + row_of(vec_ref, 3))
+    h = start[rows, :].astype(F32) + (mm_nt(att[rows, :], item(all_w, PROJ)) + row_of(vec, V_PROJ))
     xhat, _ = norm_parts(h)
-    first = xhat * row_of(vec_ref, 4) + row_of(vec_ref, 5)
-    low_ref[rows, :] = first.astype(BF16)
-    first_ref[rows, :] = first + row_of(vec_ref, 6)
-
-def ff_part(s, i, size, low_ref, w1_ref, w2_ref, vec_ref, acc_ref):
+    first = xhat * row_of(vec, V_GAIN1) + row_of(vec, V_SHIFT1)
+    low[rows, :] = first.astype(BF16)
+    acc[rows, :] = first + row_of(vec, V_OUTER)
+
+def ff_part(j, i, size, low, all_w, vec, acc):
     rows = pl.ds(pl.multiple_of(i * size, size), size)
-    x = mm(low_ref[rows, :], w1_ref[s]) + vec_ref[s, 0:1, :].astype(F32)
+    x = mm_nt(low[rows, :], item(all_w, INNER + j)) + row_of(vec, j)
     a = jnp.abs(x)
     q, _ = upper_tail(a)
     active = (jnp.maximum(x, 0.0) - a * q).astype(BF16)
-    acc_ref[rows, :] += mm(active, w2_ref[s])
-
-def out_norm(i, size, acc_ref, vec_ref, out_ref):
+    acc[rows, :] += mm(active, item(all_w, OUTER + j))
+
+def out_norm(i, size, acc, vec, out):
     rows = pl.ds(pl.multiple_of(i * size, size), size)
-    xhat, _ = norm_parts(acc_ref[rows, :])
-    out_ref[rows, :] = (xhat * row_of(vec_ref, 7) + row_of(vec_ref, 8)).astype(BF16)
-
-def fwd_kernel(tokens, idf, tab, wt, wpt, w1, w2, vec, out, start, att, qkvt, colb, acc, low):
+    xhat, _ = norm_parts(acc[rows, :])
+    out[rows, :] = (xhat * row_of(vec, V_GAIN2) + row_of(vec, V_SHIFT2)).astype(BF16)
+
+def fwd_kernel(tokens, masked, ids, tab_own, qkv_own, proj_own, inner_own, outer_own, *rest):
+    smalls, rest = rest[:9], rest[9:]
+    (out, start, att, qkvt, w_out, vec, idf,
+     all_w, parts, colb, acc, low, send_sem, recv_sem, vsend, vrecv, own_sem, out_sem) = rest
     T = tokens.shape[0]
     pages = T // SEQ
+    dp, fs = lax.axis_index("dp"), lax.axis_index("fsdp")
+    y, c = fs // 2, fs % 2
+    x, z = dp % 2, (dp // 2) % 2
+    to_c, to_y = (dp, 2 * y + 1 - c), (dp, 2 * (1 - y) + c)
+    to_x, to_z = (dp + 1 - 2 * x, fs), (dp + 2 - 4 * z, fs)
+    across = 2 * (1 - y) + c
+    part = PART // 4
+    spot = [part * (x + 2 * z), part * (1 - x + 2 * z), part * (x + 2 * (1 - z)), part * (1 - x + 2 * (1 - z))]
+
+    def rows_of(m, s, at=0, size=PART):
+        return pl.ds(pl.multiple_of(m * D + PART * s + at, 16), size)
+
+    own_copies = []
+    for src, m, count in ((tab_own, TAB, 1), (qkv_own, QKV, 3), (proj_own, PROJ, 1), (outer_own, OUTER, 4)):
+        for j in range(count):
+            own_copies.append(pltpu.make_async_copy(src.at[pl.ds(PART * j, PART)], all_w.at[rows_of(m + j, fs)], own_sem.at[len(own_copies)]))
+    for k in own_copies:
+        k.start()
+    idf[...] = jnp.where(masked[...] > 0, ids[...], -1).astype(F32)
+    place_vectors(fs, smalls, parts)
+
+    barrier = pltpu.get_barrier_semaphore()
+    for to in (to_c, to_y, to_x, to_z):
+        pl.semaphore_signal(barrier, inc=1, device_id=to, device_id_type=MESH)
+    pl.semaphore_wait(barrier, 4)
+
+    first, second = 2 * part // 3, part // 3
+    kinds = [
+        (0, PART, fs, to_c), (spot[0], part, fs, to_y),
+        (spot[0], part, across, to_x), (spot[0], part, across, to_z), (spot[0], part, across, to_c),
+        (spot[1], part, across, to_c), (spot[1] + first, second, across, to_z),
+        (spot[2], part, across, to_c), (spot[2], first, across, to_x),
+        (spot[3], first, across, to_c), (spot[3] + first, second, across, to_c),
+    ]
+
+    def copy(m, k):
+        at, size, owner, to = kinds[k]
+        rows = rows_of(m, owner, at, size)
+        return pltpu.make_async_remote_copy(src_ref=all_w.at[rows], dst_ref=all_w.at[rows], send_sem=send_sem.at[m, k], recv_sem=recv_sem.at[m, k],
+                                            device_id=to, device_id_type=MESH)
+
+    def begin(m):
+        if m == TAB:
+            own_copies[0].wait()
+        if m == QKV:
+            for k in range(1, 5):
+                own_copies[k].wait()
+        if m == INNER:
+            flipped = inner_own[...].T
+            for j in range(4):
+                all_w[rows_of(INNER + j, fs), :] = flipped[PART * j:PART * j + PART]
+        if m >= OUTER:
+            own_copies[5 + m - OUTER].wait()
+        copy(m, 1).start()
+        copy(m, 0).start()
+
+    def from_y(m):
+        copy(m, 1).wait_recv()
+        for k in (2, 3, 4):
+            copy(m, k).start()
+
+    def from_sides(m):
+        copy(m, 2).wait_recv()
+        copy(m, 6).start()
+        copy(m, 5).start()
+        copy(m, 3).wait_recv()
+        copy(m, 8).start()
+        copy(m, 7).start()
+
+    def from_corner(m):
+        copy(m, 8).wait_recv()
+        copy(m, 9).start()
+        copy(m, 6).wait_recv()
+        copy(m, 10).start()
+
+    leave = lambda m: pltpu.make_async_copy(all_w.at[pl.ds(m * D, D)], w_out.at[pl.ds(m * D, D)], out_sem.at[m])
+
+    def complete(m):
+        for k in (0, 4, 5, 7, 9, 10):
+            copy(m, k).wait_recv()
+        if m != TAB:
+            leave(m).start()
+
+    def vec_copy(k):
+        rows = parts.at[fs] if k < 2 else parts.at[across]
+        return pltpu.make_async_remote_copy(src_ref=rows, dst_ref=rows, send_sem=vsend.at[k], recv_sem=vrecv.at[k], device_id=(to_y, to_c, to_c)[k], device_id_type=MESH)
+
+    begin(0)
+    vec_copy(0).start()
+    vec_copy(1).start()
+    begin(1)
+    begin(2)
+    begin(3)
+    from_y(0)
+    vec_copy(0).wait_recv()
+    vec_copy(2).start()
+    begin(4)
+    from_y(1)
+    from_sides(0)
+    from_y(2)
+    from_sides(1)
+    from_corner(0)
+    vec_copy(1).wait_recv()
+    vec_copy(2).wait_recv()
+    sum_vectors(parts, vec)
     make_colbias(vec, colb)
-    embed_rows(idf, tokens, tab, start)
-    @pl.loop(0, 9)
-    def _(o):
-        qkv_rows(o * 256, 256, wt, start, colb, qkvt)
+    complete(0)
+    embed_rows(idf, tokens, all_w, start)
+    begin(5)
+    for j in range(3):
+        from_y(3 + j)
+        from_sides(2 + j)
+        from_corner(1 + j)
+        complete(1 + j)
+        begin(6 + j)
+        qkv_item(j, all_w, start, colb, qkvt)
+
     @pl.loop(0, pages * 6)
     def _(it):
+        for m in range(PROJ, ITEMS):
+            for stage, first, when in ((complete, PROJ, m - 1), (from_corner, PROJ, m - 2), (from_sides, PROJ + 1, m - 4), (from_y, PROJ + 2, m - 6), (begin, PROJ + 5, m - 9)):
+                if m >= first:
+                    @pl.when(it == when)
+                    def _():
+                        stage(m)
         attend_pair(it // 6, it % 6, qkvt, att)
+
     @pl.loop(0, T // 256)
     def _(i):
-        proj_norm(i, 256, att, wpt, start, vec, acc, low)
+        proj_norm(i, 256, att, all_w, start, vec, acc, low)
     @pl.loop(0, 4 * (T // 512))
     def _(it):
-        ff_part(it // (T // 512), it % (T // 512), 512, low, w1, w2, vec, acc)
+        ff_part(it // (T // 512), it % (T // 512), 512, low, all_w, vec, acc)
     @pl.loop(0, T // 256)
     def _(i):
         out_norm(i, 256, acc, vec, out)
-
-def forward_call(tokens, idf, tab, wt, wpt, w1, w2, vec):
+    for m in range(ITEMS):
+        for k in range(len(kinds)):
+            copy(m, k).wait_send()
+        if m != TAB:
+            leave(m).wait()
+    for k in range(3):
+        vec_copy(k).wait_send()
+
+def forward_call(tokens, masked, ids, tab, qkv, proj, inner, outer, smalls):
     T = tokens.shape[0]
     vm = pl.BlockSpec(memory_space=pltpu.VMEM)
+    hb = pl.BlockSpec(memory_space=pl.ANY)
+    shp = jax.ShapeDtypeStruct
+    dma = pltpu.SemaphoreType.DMA
     return pl.pallas_call(
         fwd_kernel,
-        out_shape=[jax.ShapeDtypeStruct((T, D), BF16), jax.ShapeDtypeStruct((T, D), BF16), jax.ShapeDtypeStruct((T, D), BF16), jax.ShapeDtypeStruct((3 * D, T), BF16)],
-        in_specs=[vm] * 8, out_specs=[vm] * 4,
-        scratch_shapes=[pltpu.VMEM((3 * D, 128), F32), pltpu.VMEM((T, D), F32), pltpu.VMEM((T, D), BF16)],
-        compiler_params=pltpu.CompilerParams(vmem_limit_bytes=60 * 2**20), name="forward",
-    )(tokens, idf, tab, wt, wpt, w1, w2, vec)
-
-
-ROWS_OUTER, ROWS_INNER, ROWS_PROJ, ROWS_QKV, ROWS_TABLE, ROWS_VEC = 0, 768, 1536, 1728, 2304, 2496
-ROWS = 2560
+        out_shape=[shp((T, D), BF16), shp((T, D), BF16), shp((T, D), BF16), shp((3 * D, T), BF16), shp((ITEMS * D, D), BF16), shp((12, 8, D), F32), shp((T // 128, 128), F32)],
+        in_specs=[vm, vm, vm, hb, hb, hb, vm, hb] + [vm] * 9, out_specs=[vm] * 4 + [hb, vm, vm],
+        scratch_shapes=[pltpu.VMEM((ITEMS * D, D), BF16), pltpu.VMEM((4, 16, D), BF16), pltpu.VMEM((3 * D, 128), F32), pltpu.VMEM((T, D), F32), pltpu.VMEM((T, D), BF16),
+                        dma((ITEMS, 11)), dma((ITEMS, 11)), dma((3,)), dma((3,)), dma((9,)), dma((ITEMS,))],
+        compiler_params=pltpu.CompilerParams(collective_id=0, has_side_effects=True, vmem_limit_bytes=60 * 2**20), name="forward",
+    )(tokens, masked, ids, tab, qkv, proj, inner, outer, *smalls)
+
+
 HALF = 128
+VEC_ROWS = 64
 
 def mm_tn(a, b):
     return mm(a.T, b)
@@ -158,90 +314,100 @@
     else:
         ref[index] = (ref[index].astype(F32) + value).astype(ref.dtype)
 
-def bwd_kernel(nb_ref, idf, start_h, att_h, cot_h, qkvt_h, wt_h, wpt_h, w1_h, w2_h, vec_h, grad_h, token_h,
-               start, att, cot, qkvt, wpt, w1, w2, vec, grad, tok,
-               active, slope, low, acc, xhat_one, g_first, qct, gact, gone, gqc, gkv, gall, sums, pick, rank, sem_in, sem_out):
+def add(sums, k, values):
+    sums[k] += jnp.sum(values.reshape(-1, 8, values.shape[-1]), axis=0)
+
+def item_row(row):
+    block = row // PART
+    return ((block % 3) * 4 + block // 3) * PART + row % PART
+
+def split(v):
+    high = v.astype(BF16)
+    return high, (v - high.astype(F32)).astype(BF16)
+
+def bwd_kernel(idf, vec, out_h, start_h, att_h, cot_h, qkvt_h, w_h, grad_h, gvec, token_h, layer_out,
+               start, att, cot, qkvt, w, grad, tok, active, slope, low, acc, xhat_one, g_first, qct, gact, gone, gqt, sums, pick, rank, stage, tacc, sem_in, sem_out):
     T = start.shape[0]
     pages = T // SEQ
-    W = pages * HALF
+    per = SEQ // 128
+    base = PROJ
+    span = lambda a, b: (w_h.at[pl.ds(a * D, (b - a) * D)], w.at[pl.ds((a - base) * D, (b - a) * D)])
     arrivals = {}
-    for k, (name, src, dst) in enumerate((("vec", vec_h, vec), ("start", start_h, start), ("att", att_h, att), ("wpt", wpt_h, wpt), ("w1", w1_h, w1), ("w2", w2_h, w2),
-                                          ("cot", cot_h, cot), ("qkvt", qkvt_h, qkvt))):
+    for k, (name, src, dst) in enumerate((("start", start_h, start), ("att", att_h, att), ("proj",) + span(PROJ, INNER), ("inner",) + span(INNER, OUTER),
+                                          ("outer",) + span(OUTER, ITEMS), ("cot", cot_h, cot), ("qkvt", qkvt_h, qkvt))):
         arrivals[name] = pltpu.make_async_copy(src, dst, sem_in.at[k])
         arrivals[name].start()
+    weight = lambda m: item(w, m - base)
+    pass_on = pltpu.make_async_copy(out_h, layer_out, sem_in.at[8])
+    pass_on.start()
 
     r_i = lax.broadcasted_iota(jnp.int32, (SEQ, SEQ), 0)
     c_i = lax.broadcasted_iota(jnp.int32, (SEQ, SEQ), 1)
     upper = (r_i < c_i).astype(F32).astype(BF16)
-    per = SEQ // 128
     for p in range(pages):
         ids = jnp.concatenate([idf[per * p + k:per * p + k + 1, :] for k in range(per)], axis=1)
         ids8 = jnp.broadcast_to(ids, (8, SEQ))
         hit = (ids8 >= 0.0).astype(F32)
         before = mm(jnp.concatenate([hit, hit], axis=0).astype(BF16), upper)[:8]
         rank[p] = jnp.where(ids8 >= 0.0, before, -1e6)
-
     sums[...] = jnp.zeros_like(sums)
     row_j = lax.broadcasted_iota(jnp.int32, (HALF, SEQ), 0).astype(F32)
 
-    def make_pick(b):
-        for p in range(pages):
-            want = row_j + (b * HALF).astype(F32) if not isinstance(b, int) else row_j + float(b * HALF)
-            pick[p] = (jnp.broadcast_to(rank[p][0:1, :], (HALF, SEQ)) == want).astype(F32).astype(BF16)
-
     def picked(ref):
         return jnp.concatenate([mm(pick[p], ref[p * SEQ:(p + 1) * SEQ, :]) for p in range(pages)], axis=0)
 
     def block(b, first):
         wait = (lambda n: arrivals[n].wait()) if first else (lambda n: None)
-        make_pick(b)
-        wait("start"); wait("att"); wait("vec"); wait("wpt")
-        start_c = picked(start)
+        offset = float(b * HALF) if first else (b * HALF).astype(F32)
+        for p in range(pages):
+            pick[p] = (jnp.broadcast_to(rank[p][0:1, :], (HALF, SEQ)) == row_j + offset).astype(F32).astype(BF16)
+        wait("start"); wait("att"); wait("proj")
         att_c = picked(att).astype(BF16)
-        h = start_c + (mm_nt(att_c, wpt[...]) + row_of(vec, 3))
+        h = picked(start) + (mm_nt(att_c, weight(PROJ)) + row_of(vec, V_PROJ))
         xhat, inv_one = norm_parts(h)
         xhat_one[...] = xhat
-        f = xhat * row_of(vec, 4) + row_of(vec, 5)
+        f = xhat * row_of(vec, V_GAIN1) + row_of(vec, V_SHIFT1)
         low[...] = f.astype(BF16)
-        acc[...] = f + row_of(vec, 6)
-        wait("w1"); wait("w2")
+        acc[...] = f + row_of(vec, V_OUTER)
+        wait("inner"); wait("outer")
         @pl.loop(0, 4)
-        def _(s):
-            x = mm(low[...], w1[s]) + vec[s, 0:1, :].astype(F32)
+        def _(j):
+            x = mm_nt(low[...], weight(INNER + j)) + row_of(vec, j)
             a = jnp.abs(x)
             q, bell = upper_tail(a)
-            active[s] = (jnp.maximum(x, 0.0) - a * q).astype(BF16)
-            slope[s] = (jnp.where(x >= 0.0, 1.0 - q, q) + x * (bell * 0.3989422804014327)).astype(BF16)
-            acc[...] += mm(active[s], w2[s])
+            active[j] = (jnp.maximum(x, 0.0) - a * q).astype(BF16)
+            slope[j] = (jnp.where(x >= 0.0, 1.0 - q, q) + x * (bell * 0.3989422804014327)).astype(BF16)
+            acc[...] += mm(active[j], weight(OUTER + j))
         xhat_two, inv_two = norm_parts(acc[...])
         wait("cot")
         g_out = picked(cot)
-        sums[9:10, :] += jnp.sum(g_out * xhat_two, axis=0, keepdims=True)
-        sums[10:11, :] += jnp.sum(g_out, axis=0, keepdims=True)
-        g_two = norm_back(xhat_two, inv_two, row_of(vec, 7), g_out)
+        add(sums, V_GAIN2, g_out * xhat_two)
+        add(sums, V_SHIFT2, g_out)
+        g_two = norm_back(xhat_two, inv_two, row_of(vec, V_GAIN2), g_out)
         g_outer = g_two.astype(BF16)
-        sums[8:9, :] += jnp.sum(g_outer.astype(F32), axis=0, keepdims=True)
+        add(sums, V_OUTER, g_outer.astype(F32))
         g_first[...] = g_two
-        low_t = low[...].T
         @pl.loop(0, 4)
-        def _(s):
-            put(grad, (s, pl.ds(ROWS_OUTER, D)), mm_tn(active[s], g_outer), first)
-            g_inner = (mm_nt(g_outer, w2[s]) * slope[s].astype(F32)).astype(BF16)
-            sums[pl.ds(s, 1), :] += jnp.sum(g_inner.astype(F32), axis=0, keepdims=True)
-            put(grad, (s, pl.ds(ROWS_INNER, D)), mm(low_t, g_inner), first)
-            g_first[...] += mm_nt(g_inner, w1[s])
+        def _(j):
+            put(grad, (pl.ds(pl.multiple_of((OUTER + j) * D, D), D),), mm_tn(active[j], g_outer), first)
+            g_inner = (mm_nt(g_outer, weight(OUTER + j)) * slope[j].astype(F32)).astype(BF16)
+            add(sums, j, g_inner.astype(F32))
+            put(grad, (pl.ds(pl.multiple_of((INNER + j) * D, D), D),), mm_tn(g_inner, low[...]), first)
+            g_first[...] += mm(g_inner, weight(INNER + j))
         g = g_first[...]
         xhat = xhat_one[...]
-        sums[6:7, :] += jnp.sum(g * xhat, axis=0, keepdims=True)
-        sums[7:8, :] += jnp.sum(g, axis=0, keepdims=True)
-        g_one = norm_back(xhat, inv_one, row_of(vec, 4), g)
-        gone[b] = g_one
-        g_proj = g_one.astype(BF16)
-        sums[5:6, :] += jnp.sum(g_proj.astype(F32), axis=0, keepdims=True)
-        dwp = mm_tn(g_proj, att_c)
-        for s in range(4):
-            put(grad, (s, pl.ds(ROWS_PROJ, 192)), dwp[192 * s:192 * s + 192], first)
-        gact[...] = mm(g_proj, wpt[...]).astype(BF16).T
+        add(sums, V_GAIN1, g * xhat)
+        add(sums, V_SHIFT1, g)
+        g_one = norm_back(xhat, inv_one, row_of(vec, V_GAIN1), g)
+        high, rest = split(g_one)
+        for p in range(pages):
+            back = pick[p].T
+            mine = slice(p * HALF, (p + 1) * HALF)
+            put(gone, (slice(p * SEQ, (p + 1) * SEQ),), mm(back, high[mine]) + mm(back, rest[mine]), first)
+        g_proj = high
+        add(sums, V_PROJ, g_proj.astype(F32))
+        put(grad, (pl.ds(PROJ * D, D),), mm_tn(g_proj, att_c), first)
+        gact[...] = mm(g_proj, weight(PROJ)).astype(BF16).T
         wait("qkvt")
         for p in range(pages):
             qct[:, p * HALF:(p + 1) * HALF] = mm_nt(qkvt[0:D, p * SEQ:(p + 1) * SEQ], pick[p]).astype(BF16)
@@ -253,6 +419,7 @@
             for sub in range(2):
                 head = pair * 2 + sub
                 at = lambda part: pl.ds(pl.multiple_of(part * D + head * HEAD, HEAD), HEAD)
+                to = lambda part: pl.ds(pl.multiple_of(item_row(part * D + head * HEAD), HEAD), HEAD)
                 kt = qkvt[at(1), cols]
                 vn = qkvt[at(2), cols].T
                 qt = qct[at(0), small]
@@ -264,104 +431,98 @@
                 gp = mm(vn, ga)
                 d = jnp.sum(p * gp, axis=0, keepdims=True)
                 gs = (p * (gp - d) * HEAD ** -0.5).astype(BF16)
-                gqc[b, at(0), small] = mm(kt, gs).astype(BF16)
-                put(gkv, (at(0), cols), mm_nt(qt, gs), first)
-                put(gkv, (at(1), cols), mm_nt(ga, p.astype(BF16)), first)
-        dwq = mm(gqc[b], start_c.astype(BF16))
-        put(grad, (0, pl.ds(ROWS_QKV, 576)), dwq[:576], first)
-        put(grad, (1, pl.ds(ROWS_QKV, 192)), dwq[576:], first)
-        ones = jnp.ones((16, W), BF16)
-        sums[4:5, :] += mm_nt(ones, gqc[b])[0:1]
-
-    def table_block(b, first):
-        make_pick(b)
-        gall[0:D, :] = gqc[b]
-        hots = []
-        for p in range(pages):
-            gall[D:3 * D, p * HALF:(p + 1) * HALF] = mm_nt(gkv[:, p * SEQ:(p + 1) * SEQ], pick[p]).astype(BF16)
-            ids = jnp.concatenate([idf[per * p + k:per * p + k + 1, :] for k in range(per)], axis=1)
-            hot = (jnp.broadcast_to(ids, (TABLE, SEQ)) == lax.broadcasted_iota(jnp.int32, (TABLE, SEQ), 0).astype(F32)).astype(F32).astype(BF16)
-            hots.append(mm_nt(hot, pick[p]).astype(BF16))
-        gt = gall[...].T
-        g_start = gone[b] + sum(mm(gt[:, D * k:D * k + D], w2[k]) for k in range(3))
-        dtab = mm(jnp.concatenate(hots, axis=1), g_start.astype(BF16))
-        for s in range(4):
-            put(grad, (s, pl.ds(ROWS_TABLE, 192)), dtab[192 * s:192 * s + 192], first)
-
-    nb = nb_ref[0]
+                put(gqt, (to(0), cols), mm(mm(kt, gs).astype(BF16), pick[page]), first)
+                put(gqt, (to(1), cols), mm_nt(qt, gs), first)
+                put(gqt, (to(2), cols), mm_nt(ga, p.astype(BF16)), first)
+
+    most = functools.reduce(jnp.maximum, [jnp.sum((idf[per * p:per * p + per, :] >= 0.0).astype(F32)) for p in range(pages)])
+    nb = (most.astype(jnp.int32) + HALF - 1) // HALF
     block(0, True)
     @pl.loop(1, nb)
     def _(b):
         block(b, False)
-    outs = []
-    def send(k, src, dst):
-        c = pltpu.make_async_copy(src, dst, sem_out.at[k]); c.start(); outs.append(c)
-    for s in range(4):
-        send(s, grad.at[s, pl.ds(0, ROWS_QKV)], grad_h.at[s, pl.ds(0, ROWS_QKV)])
-    wt_copy = pltpu.make_async_copy(wt_h, w2.at[pl.ds(0, 3)], sem_in.at[8])
-    wt_copy.start()
-    @pl.loop(0, 8)
-    def _(i):
-        o = 192 * i
-        at = D + o
-        grad[at // 576, pl.ds(pl.multiple_of(ROWS_QKV + at % 576, 64), 192)] = mm(gkv[pl.ds(pl.multiple_of(o, 64), 192), :], start[...]).astype(BF16)
-    sums[11:12, :] += mm_nt(jnp.ones((16, T), BF16), gkv[D:2 * D, :])[0:1]
-    wt_copy.wait()
-    table_block(0, True)
-    @pl.loop(1, nb)
-    def _(b):
-        table_block(b, False)
-    for s in range(4):
-        rest = jnp.concatenate([sums[4:12, :], jnp.zeros((7, D), F32)], axis=0)
-        grad[s, ROWS_VEC:ROWS_VEC + 16, :] = jnp.concatenate([sums[s:s + 1, :], rest], axis=0).astype(BF16)
-        grad[s, ROWS_VEC + 16:ROWS, :] = jnp.zeros((ROWS - ROWS_VEC - 16, D), BF16)
-        send(4 + s, grad.at[s, pl.ds(ROWS_QKV, ROWS - ROWS_QKV)], grad_h.at[s, pl.ds(ROWS_QKV, ROWS - ROWS_QKV)])
+
+    qkv_w = pltpu.make_async_copy(w_h.at[pl.ds(QKV * D, 3 * D)], w.at[pl.ds((OUTER - base) * D, 3 * D)], sem_in.at[7])
+    qkv_w.start()
+    early = pltpu.make_async_copy(grad.at[pl.ds(PROJ * D, (ITEMS - PROJ) * D)], grad_h.at[pl.ds(PROJ * D, (ITEMS - PROJ) * D)], sem_out.at[0])
+    early.start()
+    @pl.loop(0, 3)
+    def _(j):
+        rows = pl.ds(pl.multiple_of(j * D, D), D)
+        grad[pl.ds(pl.multiple_of((QKV + j) * D, D), D), :] = mm(gqt[rows, :], start[...]).astype(BF16)
+    middle = pltpu.make_async_copy(grad.at[pl.ds(QKV * D, 3 * D)], grad_h.at[pl.ds(QKV * D, 3 * D)], sem_out.at[1])
+    middle.start()
+    stage[...] = jnp.zeros_like(stage)
+    for k in range(12):
+        stage[k:k + 1, :] = jnp.sum(sums[k], axis=0, keepdims=True)
+    ones = jnp.ones((16, T), BF16)
+    for k, part in ((12, 0), (16, 2)):
+        for i in range(4):
+            at = item_row(part * D + PART * i)
+            stage[k + i:k + i + 1, 0:PART] = mm_nt(ones, gqt[at:at + PART, :])[0:1]
+    gvec[...] = stage[...].astype(BF16)
+    qkv_w.wait()
+    tacc[...] = jnp.zeros_like(tacc)
+    r_i = lax.broadcasted_iota(jnp.int32, (TABLE, 256), 0).astype(F32)
+    def leave(i, slot):
+        rows = pl.ds(i * 256 if isinstance(i, int) else pl.multiple_of(i * 256, 256), 256)
+        return pltpu.make_async_copy(tok.at[slot], token_h.at[rows], sem_out.at[2 + slot])
     @pl.loop(0, T // 256)
     def _(i):
         rows = pl.ds(pl.multiple_of(i * 256, 256), 256)
-        gt = gkv[:, rows].T
-        g = mm(gt[:, :D], w2[1]) + mm(gt[:, D:], w2[2])
+        gt = gqt[:, rows].T
+        g = gone[rows, :]
+        for j in range(3):
+            g = g + mm(gt[:, D * j:D * j + D], item(w, OUTER - base + j))
         slot = i % 2
         @pl.when(i >= 2)
         def _():
-            pltpu.make_async_copy(tok.at[slot], token_h.at[pl.ds(pl.multiple_of(i * 256 - 512, 256), 256)], sem_out.at[8 + slot]).wait()
+            leave(i - 2, slot).wait()
+        lows = []
         for k in range(2):
             ids = jnp.broadcast_to(idf[pl.ds(2 * i + k, 1), :], (128, 128)).T
             kept = jnp.concatenate([ids] * (D // 128), axis=1) < 0.0
-            tok[slot, 128 * k:128 * k + 128, :] = jnp.where(kept, g[128 * k:128 * k + 128], 0.0)
-        pltpu.make_async_copy(tok.at[slot], token_h.at[rows], sem_out.at[8 + slot]).start()
-    for c in outs: c.wait()
+            here = g[128 * k:128 * k + 128]
+            tok[slot, 128 * k:128 * k + 128, :] = jnp.where(kept, here, 0.0)
+            lows.append(jnp.where(kept, 0.0, here).astype(BF16))
+        leave(i, slot).start()
+        ids = jnp.concatenate([idf[pl.ds(2 * i, 1), :], idf[pl.ds(2 * i + 1, 1), :]], axis=1)
+        hot = (jnp.broadcast_to(ids, (TABLE, 256)) == r_i).astype(F32).astype(BF16)
+        tacc[...] += mm(hot, jnp.concatenate(lows, axis=0))
+    grad[0:D, :] = tacc[...].astype(BF16)
+    late = pltpu.make_async_copy(grad.at[pl.ds(0, D)], grad_h.at[pl.ds(0, D)], sem_out.at[4])
+    late.start()
+    early.wait()
+    middle.wait()
     for i in range(T // 256 - 2, T // 256):
-        pltpu.make_async_copy(tok.at[i % 2], token_h.at[pl.ds(256 * i, 256)], sem_out.at[8 + i % 2]).wait()
-
-def backward_call(nb, idf, start, att, cot, qkvt, wt, wpt, w1, w2, vec):
+        leave(i, i % 2).wait()
+    late.wait()
+    pass_on.wait()
+
+def backward_call(idf, vec, out, start, att, cot, qkvt, w):
     T = start.shape[0]
     pages = T // SEQ
     W = pages * HALF
-    n = w1.shape[0]
-    top = SEQ // HALF
     vm = pl.BlockSpec(memory_space=pltpu.VMEM)
     hb = pl.BlockSpec(memory_space=pl.ANY)
-    same = lambda a: pltpu.VMEM(a.shape, a.dtype)
+    f32 = lambda *s: pltpu.VMEM(s, F32)
+    low = lambda *s: pltpu.VMEM(s, BF16)
     return pl.pallas_call(
         bwd_kernel,
-        out_shape=[jax.ShapeDtypeStruct((n, ROWS, D), BF16), jax.ShapeDtypeStruct((T, D), F32)],
-        in_specs=[pl.BlockSpec(memory_space=pltpu.SMEM), vm] + [hb] * 9, out_specs=[hb] * 2,
-        scratch_shapes=[same(a) for a in (start, att, cot, qkvt, wpt, w1, w2, vec)] + [
-            pltpu.VMEM((n, ROWS, D), BF16), pltpu.VMEM((2, 256, D), F32),
-            pltpu.VMEM((n, W, D), BF16), pltpu.VMEM((n, W, D), BF16), pltpu.VMEM((W, D), BF16), pltpu.VMEM((W, D), F32), pltpu.VMEM((W, D), F32), pltpu.VMEM((W, D), F32),
-            pltpu.VMEM((D, W), BF16), pltpu.VMEM((D, W), BF16), pltpu.VMEM((top, W, D), F32), pltpu.VMEM((top, D, W), BF16),
-            pltpu.VMEM((2 * D, T), BF16), pltpu.VMEM((3 * D, W), BF16), pltpu.VMEM((16, D), F32), pltpu.VMEM((pages, HALF, SEQ), BF16), pltpu.VMEM((pages, 8, SEQ), F32),
-            pltpu.SemaphoreType.DMA((9,)), pltpu.SemaphoreType.DMA((10,))],
+        out_shape=[jax.ShapeDtypeStruct((ITEMS * D, D), BF16), jax.ShapeDtypeStruct((VEC_ROWS, D), BF16), jax.ShapeDtypeStruct((T, D), F32), jax.ShapeDtypeStruct((T, D), BF16)],
+        in_specs=[vm, vm] + [hb] * 6, out_specs=[hb, vm, hb, hb],
+        scratch_shapes=[low(T, D), low(T, D), low(T, D), low(3 * D, T), low((ITEMS - PROJ) * D, D), low(ITEMS * D, D), f32(2, 256, D),
+                        low(4, W, D), low(4, W, D), low(W, D), f32(W, D), f32(W, D), f32(W, D), low(D, W), low(D, W), f32(T, D), low(3 * D, T),
+                        f32(12, 8, D), low(pages, HALF, SEQ), f32(pages, 8, SEQ), f32(VEC_ROWS, D), f32(TABLE, D),
+                        pltpu.SemaphoreType.DMA((9,)), pltpu.SemaphoreType.DMA((5,))],
         compiler_params=pltpu.CompilerParams(vmem_limit_bytes=62 * 2**20), name="backward",
-    )(nb, idf, start, att, cot, qkvt, wt.reshape(3, D, D), wpt, w1, w2, vec)
-
-
-MESH = pl.DeviceIdType.MESH
+    )(idf, vec, out, start, att, cot, qkvt, w)
+
+
 CHUNK = 64
 LAGS = (0, 2, 4, 6, 8, 10, 12)
 
-def reduce_kernel(grad, fin_h, own, rc, sy, ry, kx, sx, rx, kz, sz, rz, se, re, fin, send_sem, recv_sem, own_sem, out_sem):
+def reduce_kernel(grad, gvec, fin_h, own, rc, sy, ry, kx, sx, rx, kz, sz, rz, se, re, fin, send_sem, recv_sem, own_sem, out_sem, vsend, vrecv):
     dp, fs = lax.axis_index("dp"), lax.axis_index("fsdp")
     y, c = fs // 2, fs % 2
     x, za, zb = dp % 2, (dp // 2) % 2, dp // 4
@@ -386,7 +547,7 @@
     def remote(stage, k, src, dst, to):
         return pltpu.make_async_remote_copy(src_ref=src, dst_ref=dst, send_sem=send_sem.at[stage, k], recv_sem=recv_sem.at[stage, k], device_id=to, device_id_type=MESH)
     copies = [
-        lambda k: remote(0, k, grad.at[:, 1 - c, rows(k), :], rc.at[:, rows(k), :], to_c),
+        None,
         lambda k: remote(1, k, sy.at[rows(k)], ry.at[rows(k)], to_y),
         lambda k: remote(2, k, sx.at[hrows(k)], rx.at[hrows(k)], to_x),
         lambda k: remote(3, k, sz.at[qrows(k)], rz.at[qrows(k)], to_a),
@@ -394,17 +555,34 @@
         lambda k: remote(5, k, fin.at[quarter(k, x, za)], fin.at[quarter(k, x, za)], to_a),
         lambda k: remote(6, k, fin.at[half(k, x)], fin.at[half(k, x)], to_x),
     ]
-    local = lambda k: pltpu.make_async_copy(grad.at[:, c, rows(k), :], own.at[:, rows(k), :], own_sem.at[k])
+    per = PART // CHUNK
+    chunk_of = lambda k, side: grad.at[ITEMS - 1 - k // per, :, side, pl.ds(pl.multiple_of((k % per) * CHUNK, CHUNK), CHUNK), :]
+    copies[0] = lambda k: remote(0, k, chunk_of(k, 1 - c), rc.at[:, rows(k), :], to_c)
+    local = lambda k: pltpu.make_async_copy(chunk_of(k, c), own.at[:, rows(k), :], own_sem.at[k])
+    last = n - 1
+    both = lambda ref: [(ref.at[s, pl.ds(last * CHUNK, CHUNK)], s) for s in range(2)]
+    vec_local = [pltpu.make_async_copy(gvec, dst, own_sem.at[last + s]) for dst, s in both(own)]
+    vec_remote = [pltpu.make_async_remote_copy(src_ref=gvec, dst_ref=dst, send_sem=vsend.at[s], recv_sem=vrecv.at[s], device_id=to_c, device_id_type=MESH) for dst, s in both(rc)]
     leave = lambda k: pltpu.make_async_copy(fin.at[rows(k)], fin_h.at[rows(k)], out_sem.at[k])
 
-    @pl.loop(0, n)
+    for copy in vec_local + vec_remote:
+        copy.start()
+    @pl.loop(0, last)
     def _(k):
         copies[0](k).start()
         local(k).start()
 
     def on_y(k):
-        copies[0](k).wait_recv()
-        local(k).wait()
+        @pl.when(k < last)
+        def _():
+            copies[0](k).wait_recv()
+            local(k).wait()
+        @pl.when(k == last)
+        def _():
+            for copy in vec_local:
+                copy.wait()
+            for copy in vec_remote:
+                copy.wait_recv()
         sy[rows(k), :] = (f(own[1 - y, rows(k), :]) + f(rc[1 - y, rows(k), :])).astype(BF16)
         copies[1](k).start()
 
@@ -450,64 +628,96 @@
 
     @pl.loop(0, n)
     def _(k):
-        for copy in copies:
+        for copy in copies[1:]:
             copy(k).wait_send()
+        @pl.when(k < last)
+        def _():
+            copies[0](k).wait_send()
         leave(k).wait()
-
-def reduce_call(grad):
-    R = grad.shape[1]
+    for copy in vec_remote:
+        copy.wait_send()
+
+def reduce_call(grad, gvec):
+    R = ITEMS * PART + VEC_ROWS
     n = R // CHUNK
     hb = pl.BlockSpec(memory_space=pl.ANY)
     low = lambda *s: pltpu.VMEM(s + (D,), BF16)
     return pl.pallas_call(
         reduce_kernel,
         out_shape=jax.ShapeDtypeStruct((R, D), BF16),
-        in_specs=[hb], out_specs=hb,
+        in_specs=[hb, pl.BlockSpec(memory_space=pltpu.VMEM)], out_specs=hb,
         scratch_shapes=[low(2, R), low(2, R), low(R), low(R), pltpu.VMEM((R // 2, D), F32), low(R // 2), low(R // 2),
                         pltpu.VMEM((R // 4, D), F32), low(R // 4), low(R // 4), low(R // 4), low(R // 4), low(R),
-                        pltpu.SemaphoreType.DMA((7, n)), pltpu.SemaphoreType.DMA((7, n)), pltpu.SemaphoreType.DMA((n,)), pltpu.SemaphoreType.DMA((n,))],
+                        pltpu.SemaphoreType.DMA((7, n)), pltpu.SemaphoreType.DMA((7, n)), pltpu.SemaphoreType.DMA((n + 1,)), pltpu.SemaphoreType.DMA((n,)), pltpu.SemaphoreType.DMA((2,)), pltpu.SemaphoreType.DMA((2,))],
         compiler_params=pltpu.CompilerParams(collective_id=1, has_side_effects=True, vmem_limit_bytes=60 * 2**20), name="reduce",
-    )(grad.reshape(2, 2, R, D))
-
-def finish_kernel(fin, outer, inner, qkv, proj, table, inner_b, *smalls):
-    outer[...] = fin[ROWS_OUTER:ROWS_INNER].astype(F32)
-    inner[...] = fin[ROWS_INNER:ROWS_PROJ].astype(F32)
-    table[...] = fin[ROWS_TABLE:ROWS_VEC].astype(F32)
-    proj[...] = fin[ROWS_PROJ:ROWS_QKV].astype(F32).T
-    qkv[...] = fin[ROWS_QKV:ROWS_TABLE].astype(F32).T
-    rows = fin[ROWS_VEC:ROWS_VEC + 16].astype(F32)
-    inner_b[...] = rows[0]
+    )(grad.reshape(ITEMS, 2, 2, PART, D), gvec)
+
+def finish_kernel(fin_h, outer_h, inner_h, qkv_h, proj_h, table_h, *rest):
+    inner_b, smalls, (fin, outer, inner, qkv, proj, table, sem_in, sem_out) = rest[0], rest[1:9], rest[9:]
+    edges = [0] + [(ITEMS - m) * PART for m in (OUTER, INNER, PROJ, QKV, TAB)] + [ITEMS * PART + VEC_ROWS]
+    spans = [pl.ds(a, b - a) for a, b in zip(edges, edges[1:])]
+    loads = [pltpu.make_async_copy(fin_h.at[r], fin.at[r], sem_in.at[k]) for k, r in enumerate(spans)]
+    for copy in loads:
+        copy.start()
+    stores = []
+    def leave(src, dst):
+        stores.append(pltpu.make_async_copy(src, dst, sem_out.at[len(stores)]))
+        stores[-1].start()
+    at = lambda m: fin[(ITEMS - 1 - m) * PART:(ITEMS - m) * PART].astype(F32)
+    loads[0].wait()
+    for j in range(4):
+        outer[PART * j:PART * j + PART, :] = at(OUTER + j)
+    leave(outer, outer_h)
+    loads[1].wait()
+    inner[...] = jnp.concatenate([at(INNER + j) for j in range(4)], axis=0).T
+    leave(inner, inner_h)
+    loads[2].wait()
+    proj[...] = at(PROJ)
+    leave(proj, proj_h)
+    loads[3].wait()
+    for j in range(3):
+        qkv[PART * j:PART * j + PART, :] = at(QKV + j)
+    leave(qkv, qkv_h)
+    loads[4].wait()
+    table[...] = at(TAB)
+    leave(table, table_h)
+    loads[5].wait()
+    rows = fin[ITEMS * PART:ITEMS * PART + VEC_ROWS].astype(F32)
     me = lax.axis_index("fsdp")
-    part = D // lax.axis_size("fsdp")
+    def mine(k):
+        return sum(jnp.where(me == s, rows[k, PART * s:PART * s + PART], 0.0) for s in range(4))
+    for j in range(4):
+        inner_b[pl.ds(PART * j, PART)] = mine(j)
     for k, ref in enumerate(smalls):
-        ref[...] = sum(jnp.where(me == s, rows[1 + k, part * s:part * s + part], 0.0) for s in range(D // part))
+        if k < 2:
+            ref[...] = sum(jnp.where(me == s, rows[12 + 4 * k + s, 0:PART], 0.0) for s in range(4))
+        else:
+            ref[...] = mine(4 + k)
+    for copy in stores:
+        copy.wait()
 
 def finish_call(fin):
     vm = pl.BlockSpec(memory_space=pltpu.VMEM)
-    part = D // lax.axis_size("fsdp")
+    hb = pl.BlockSpec(memory_space=pl.ANY)
+    shapes = [(D, D), (D, D), (3 * PART, D), (PART, D), (PART, D)]
     shp = lambda *s: jax.ShapeDtypeStruct(s, F32)
     out = pl.pallas_call(
-        finish_kernel, out_shape=[shp(D, D), shp(D, D), shp(D, 3 * part), shp(D, part), shp(part, D), shp(D)] + [shp(part)] * 8,
-        in_specs=[vm], out_specs=[vm] * 14, compiler_params=pltpu.CompilerParams(vmem_limit_bytes=40 * 2**20), name="finish")(fin)
-    return *out[:6], out[6:]
+        finish_kernel, out_shape=[shp(*s) for s in shapes] + [shp(D)] + [shp(PART)] * 8,
+        in_specs=[hb], out_specs=[hb] * 5 + [vm] * 9,
+        scratch_shapes=[pltpu.VMEM(fin.shape, BF16)] + [pltpu.VMEM(s, F32) for s in shapes] + [pltpu.SemaphoreType.DMA((6,)), pltpu.SemaphoreType.DMA((5,))],
+        compiler_params=pltpu.CompilerParams(vmem_limit_bytes=40 * 2**20), name="finish")(fin)
+    outer, inner, qkv, proj, table, inner_b = out[:6]
+    return outer, inner, qkv.T, proj.T, table, inner_b, out[6:]
 
 def local_direct(tokens, masked_rows, replace_ids, cotangent, qkv_weight, query_bias, value_bias, proj_weight, proj_bias, first_gain, first_shift,
                  inner_weight, inner_bias, outer_weight, outer_bias, second_gain, second_shift, embed_table):
-    n, me = lax.axis_size("fsdp"), lax.axis_index("fsdp")
-    gather = lambda v: lax.all_gather(v, "fsdp", axis=0, tiled=True)
-    mine = jnp.arange(D) // (D // n) == me
-    place = lambda v: jnp.where(mine, jnp.tile(v, n), 0).astype(BF16)
-    smalls = (query_bias, value_bias, proj_bias, first_gain, first_shift, outer_bias, second_gain, second_shift)
-    vec = jnp.stack([inner_bias] + [place(v) for v in smalls] + [jnp.zeros(D, BF16)] * 7)
-    tab, wt, wpt = gather(embed_table), gather(qkv_weight.T), gather(proj_weight.T)
-    w1, w2, vec = gather(inner_weight[None]), gather(outer_weight[None]), gather(vec[None])
-    idf = jnp.where(masked_rows > 0, replace_ids, -1).astype(F32).reshape(-1, 128)
-    out, start, att, qkvt = forward_call(tokens, idf, tab, wt, wpt, w1, w2, vec)
-    blocks = jnp.max((jnp.sum(masked_rows.reshape(-1, SEQ), axis=1) + HALF - 1) // HALF)[None]
-    grad, token_grad = backward_call(blocks, idf, start, att, cotangent, qkvt, wt, wpt, w1, w2, vec)
-    outer, inner, qkv, proj, table, inner_b, smalls = finish_call(reduce_call(grad))
-    q, pb, fg, fs, ob, sg, ss, v = smalls
-    return (out, token_grad, qkv, q, v, proj, pb, fg, fs, inner, inner_b, outer, ob, sg, ss, table)
+    smalls = (inner_bias, query_bias, value_bias, proj_bias, first_gain, first_shift, outer_bias, second_gain, second_shift)
+    out, start, att, qkvt, w, vec, idf = forward_call(tokens, masked_rows.reshape(-1, 128), replace_ids.reshape(-1, 128), embed_table, qkv_weight.T, proj_weight.T,
+                                                      inner_weight, outer_weight, smalls)
+    grad, gvec, token_grad, layer_out = backward_call(idf, vec, out, start, att, cotangent, qkvt, w)
+    outer, inner, qkv, proj, table, inner_b, smalls = finish_call(reduce_call(grad, gvec))
+    q, v, pb, fg, fs, ob, sg, ss = smalls
+    return (layer_out, token_grad, qkv, q, v, proj, pb, fg, fs, inner, inner_b, outer, ob, sg, ss, table)
 
 
 def plain_norm_rows(hidden, gain, shift):

time: 397 us -> 269 us (0.68)
  waiting for transfers between devices: 142 us -> 0 us
  Pallas kernels: 226 us -> 266 us
  between operations: 14 us -> 0.87 us
  blocking collectives: 6.78 us -> 0 us
    all_gather x5 -> x0, waiting for transfers between devices: 139 us -> none  [local_direct(): gather = lambda v: lax.all_gather(v, 'fsdp', axis=0, tiled=True)]
    pallas_call x3, Pallas kernels: 114 us -> 152 us  [the longest x1 91.6 us: forward_call(): pl.pallas_call(fwd_kernel, out_shape=[shp((T, D), BF16), shp((T, D), BF16...]
    all_gather x1 -> x0, blocking collectives: 6.78 us -> none  [local_direct(): gather = lambda v: lax.all_gather(v, 'fsdp', axis=0, tiled=True)]
  transfers between devices with their start and end apart: 5 -> 0, of which waited for: 5 -> 0; matrix products, arithmetic and copies ran while one was open for 1% -> 0% of each run, Pallas kernels for 0% -> 0%
where the time goes in v2:
time: 269 us
  Pallas kernels  266 us (99%)
    pallas_call x1, Pallas kernels, reduce_call(): pl.pallas_call(reduce_kernel, out_shape=jax.ShapeDtypeStruct((R, D), BF16...  113 us
    pallas_call x1, Pallas kernels, forward_call(): pl.pallas_call(fwd_kernel, out_shape=[shp((T, D), BF16), shp((T, D), BF16...  91.6 us
    pallas_call x1, Pallas kernels, backward_call(): pl.pallas_call(bwd_kernel, out_shape=[jax.ShapeDtypeStruct((ITEMS * D, D)...  55.8 us

profile of v2, /device:TPU:0, one launch (start us, length us, event | category | flops | bytes accessed | tf_op | source)
XLA Modules:
  0.0 268.7 jit_solution(15702858519549534758)
XLA Ops:
  0.7 91.6 %forward.1 = (bf16[1024,768]{1,0:T(8,128)(2,1)}, bf16[1024,768]{1,0:T(8,128)(2,1)}, bf16[1024,768]{1,0:T(8,128)(2,1)}, bf16[2304,1024]{1,0:T(8,128)(2,1)}, bf16[...) custom-call(bf16[1024,768]{1,0:T(8,128)(2,1)} %tokens.1, s32[8,128]{1,0:T(8,128)} %bitcast.10, ...), custom_call_target="tpu_custom_call" | custom-call | tf_op jit(solution)/shard_map/forward/pallas_call | solution.py:291
  92.2 55.8 %backward.1 = (bf16[9984,768]{1,0:T(8,128)(2,1)}, bf16[64,768]{1,0:T(8,128)(2,1)}, f32[1024,768]{1,0:T(8,128)}, bf16[1024,768]{1,0:T(8,128)(2,1)}) custom-call(f32[8,128]{1,0:T(8,128)} %get-tuple-element.41.idf, f32[12,8,768]{2,1,0:T(8,128)} %get-tuple-element.42.vec, bf16[1024,768]{1,0:T(8,128)(2,1)} %get-tuple-element.43.out_h, ...), custom_call_target="tpu_custom_call" | custom-call | tf_op jit(solution)/shard_map/backward/pallas_call | solution.py:510
  148.1 113.5 %reduce.1.fin_h = bf16[2560,768]{1,0:T(8,128)(2,1)} custom-call(bf16[13,2,2,192,768]{4,3,2,1,0:T(8,128)(2,1)} %bitcast.7, bf16[64,768]{1,0:T(8,128)(2,1)} %get-tuple-element.51.gvec), custom_call_target="tpu_custom_call" | custom-call | tf_op jit(solution)/shard_map/reduce/pallas_call | solution.py:645
  261.6 0.0 copy-start
  261.6 2.1 copy-done
  263.7 4.8 %finish.1 = (f32[768,768]{1,0:T(8,128)}, f32[768,768]{1,0:T(8,128)}, f32[576,768]{1,0:T(8,128)}, f32[192,768]{1,0:T(8,128)}, f32[192,768]{1,0:T(8,128)}, /*index...) custom-call(bf16[2560,768]{1,0:T(8,128)(2,1)S(1)} %copy-done), custom_call_target="tpu_custom_call" | custom-call | tf_op jit(solution)/shard_map/finish/pallas_call | solution.py:704
Async XLA Ops:
  261.6 2.1 copy-start
